TPU v7x, 32 devices: a whole 2x2x4 slice. The times are simulated.
32 devices in a mesh: comp: 4 (over y, core), tile: 8 (over z, x).
Axes of the slice: x: 2, y: 2, z: 4, core: 2. Of those that a mesh axis runs over, the one named last changes fastest.
Arguments:
- atm_u: float32 [20, 65536], P(None, ('comp', 'tile')), may hold values from -30 to 30
- atm_v: float32 [20, 65536], P(None, ('comp', 'tile')), may hold values from -30 to 30
- mixing: float32 [19, 65536], P(None, ('comp', 'tile')), may hold values from 0.05 to 5
- drag_prev: float32 [65536], P(('comp', 'tile')), may hold values from 0.01 to 0.3
- spectrum: float32 [29, 36, 65536], P(None, None, ('comp', 'tile')), may hold values from 0.01 to 1
- sea_mask: int32 [65536], P(('comp', 'tile')), may hold values 0 or 1
- wave_source: int32 [65536], P(('comp', 'tile')), may hold values from 0 to 65535, as said below
- column_target: int32 [65536], P(('comp', 'tile')), may hold values from 0 to 65535, as said below
- neighbours: int32 [4, 65536], P(None, ('comp', 'tile')), may hold values from 0 to 2175, as said below
Outputs:
- u_new: float32 [20, 65536], P(None, ('comp', 'tile'))
- v_new: float32 [20, 65536], P(None, ('comp', 'tile'))
- spectrum_new: float32 [29, 36, 65536], P(None, None, ('comp', 'tile'))
- log_roughness: float32 [65536], P(('comp', 'tile'))
- stress: float32 [65536], P(('comp', 'tile'))
Inputs may be any that keep to these rules, and one draw needn't show every extreme that they name: `wave_source`: every column is taken by exactly one wave slot; the slots of one device take exactly 64 columns of every device. The inverse of wave_source: column_target[wave_source[p]] = p. Indices into a tile extended by 64 slots on each side; a slot's west and south neighbours lie at most 64 slots before it, east and north at most 64 after it.
All inputs are finite; a program needn't handle non-finite values. No bound on the sum of `sea_mask` on one device may be relied on, other than what follows from the above.
Results may differ from a plain program's by a relative error of at most 0.0003.
Values sent between devices are 32-bit elements; how exact they have to be, the bound alone decides.
A program may use at most 128 MiB of HBM per device.

v0:
```python
import math

import jax
import jax.numpy as jnp
from jax import lax
from jax.sharding import PartitionSpec as P

HALO = 64


def extended(cells, sides, width):
    for axis, dim in sides:
        count = lax.axis_size(axis)
        head = lax.slice_in_dim(cells, 0, width, axis=dim)
        tail = lax.slice_in_dim(cells, cells.shape[dim] - width, cells.shape[dim], axis=dim)
        cells = jnp.concatenate(
            [
                lax.ppermute(tail, axis, [(i, (i + 1) % count) for i in range(count)]),
                cells,
                lax.ppermute(head, axis, [((i + 1) % count, i) for i in range(count)]),
            ],
            axis=dim,
        )
    return cells


def column_solve(old, mixing, drag):
    lev = old.shape[0]
    zero = jnp.zeros_like(old[0])
    cps = []
    dps = []
    for k in range(lev):
        above = mixing[k - 1] if k > 0 else zero
        below = mixing[k] if k < lev - 1 else zero
        diag = 1.0 + above + below
        if k == lev - 1:
            diag = diag + drag
        if k == 0:
            denom = diag
            dcur = old[k] / denom
        else:
            denom = diag - above * cps[k - 1]
            dcur = (old[k] + above * dps[k - 1]) / denom
        cps.append(-below / denom)
        dps.append(dcur)
    result = [None] * lev
    result[lev - 1] = dps[lev - 1]
    for k in range(lev - 2, -1, -1):
        result[k] = dps[k] - cps[k] * result[k + 1]
    return jnp.stack(result)


def wave_block(padded, mask, nbr, wind_u, wind_v):
    nfreq, ndir, total = padded.shape
    width = nbr.shape[1]
    rim = (total - width) // 2
    rows_all = nfreq * ndir
    flat = padded.reshape(rows_all, total)
    block_width = 128
    span = block_width + 2 * rim
    freq = 0.0418 * 1.1 ** jnp.arange(nfreq, dtype=jnp.float32)
    theta = 2.0 * math.pi * (jnp.arange(ndir, dtype=jnp.float32) + 0.5) / ndir
    courant = 0.7 * freq[0] / freq
    cx = (courant[:, None] * jnp.cos(theta)[None, :]).reshape(rows_all, 1)
    cy = (courant[:, None] * jnp.sin(theta)[None, :]).reshape(rows_all, 1)
    freq_col = jnp.repeat(freq, ndir)[:, None]
    sigma = jnp.repeat(freq / freq[nfreq - 1], ndir)[:, None]
    cos_col = jnp.tile(jnp.cos(theta), nfreq)[:, None]
    sin_col = jnp.tile(jnp.sin(theta), nfreq)[:, None]
    positions = jnp.arange(span, dtype=jnp.int32)[:, None, None]
    fmask_all = mask.astype(jnp.float32)

    def advance(index, carry):
        spec_out, logz_out, tau_out = carry
        start = (index * block_width).astype(jnp.int32)
        window = lax.dynamic_slice_in_dim(flat, start, span, 1)
        nearest = lax.dynamic_slice_in_dim(nbr, start, block_width, 1) - start
        table = (positions == nearest[None]).astype(jnp.float32).reshape(span, 4 * block_width)
        picked = jnp.dot(
            window, table, precision=lax.Precision.HIGHEST, preferred_element_type=jnp.float32
        )
        center = window[:, rim : rim + block_width]
        west = picked[:, :block_width]
        east = picked[:, block_width : 2 * block_width]
        south = picked[:, 2 * block_width : 3 * block_width]
        north = picked[:, 3 * block_width :]
        upx = jnp.where(cx > 0, west, east)
        upy = jnp.where(cy > 0, south, north)
        moved = center - jnp.abs(cx) * (center - upx) - jnp.abs(cy) * (center - upy)
        wind_east = lax.dynamic_slice_in_dim(wind_u, start, block_width, 0)
        wind_north = lax.dynamic_slice_in_dim(wind_v, start, block_width, 0)
        fmask = lax.dynamic_slice_in_dim(fmask_all, start, block_width, 0)
        speed = jnp.maximum(jnp.sqrt(wind_east * wind_east + wind_north * wind_north), 1.0)
        ustar0 = 0.035 * speed
        cosw = (wind_east[None, :] * cos_col + wind_north[None, :] * sin_col) / speed[None, :]
        gamma = jnp.maximum(0.0, 18.0 * freq_col * ustar0[None, :] * cosw - 1.0)
        energy = jnp.mean(moved, axis=0)
        growth = 1.0 + 0.3 * sigma * gamma - 0.5 * sigma * (energy / (1.0 + energy))[None, :]
        new_spec = fmask[None, :] * moved * growth
        tau_wave = fmask * jnp.mean(sigma * gamma * moved, axis=0)
        ratio = jnp.minimum(tau_wave / (ustar0 * ustar0), 0.9)
        z0 = 0.01 / jnp.sqrt(1.0 - ratio) * ustar0 * ustar0 / 9.81 + 1.5e-05
        ustar = 0.4 * speed / jnp.log(10.0 / z0)
        spec_out = lax.dynamic_update_slice_in_dim(spec_out, new_spec, start, 1)
        logz_out = lax.dynamic_update_slice_in_dim(logz_out, jnp.log(z0), start, 0)
        tau_out = lax.dynamic_update_slice_in_dim(tau_out, ustar * ustar, start, 0)
        return (spec_out, logz_out, tau_out)

    initial = (
        jnp.zeros((rows_all, width), jnp.float32),
        jnp.zeros((width,), jnp.float32),
        jnp.zeros((width,), jnp.float32),
    )
    spec_all, logz_all, tau_all = lax.fori_loop(0, width // block_width, advance, initial)
    return (spec_all.reshape(nfreq, ndir, width), logz_all, tau_all)


def local(
    atm_u, atm_v, mixing, drag_prev, spectrum, sea_mask, wave_source, column_target, neighbours
):
    columns = atm_u.shape[1]
    n_comp = lax.axis_size("comp")
    n_tile = lax.axis_size("tile")
    devices = n_comp * n_tile
    per_peer = columns // devices
    order_out = jnp.argsort(column_target // columns, stable=True)
    order_in = jnp.argsort(wave_source, stable=True)
    lowest = jnp.stack([atm_u[-1], atm_v[-1]])
    outgoing = lowest[:, order_out].reshape(2, devices, per_peer)
    incoming = lax.all_to_all(outgoing, ("comp", "tile"), split_axis=1, concat_axis=1, tiled=True)
    padded = extended(spectrum, ((("comp", "tile"), 2),), HALO)
    u_new = column_solve(atm_u, mixing, drag_prev)
    v_new = column_solve(atm_v, mixing, drag_prev)
    winds = jnp.zeros((2, columns), jnp.float32).at[:, order_in].set(incoming.reshape(2, columns))
    spectrum_new, logz, tau = wave_block(padded, sea_mask, neighbours, winds[0], winds[1])
    backward = jnp.stack([logz, tau])[:, order_in].reshape(2, devices, per_peer)
    returned = lax.all_to_all(backward, ("comp", "tile"), split_axis=1, concat_axis=1, tiled=True)
    placed = jnp.zeros((2, columns), jnp.float32).at[:, order_out].set(returned.reshape(2, columns))
    return (u_new, v_new, spectrum_new, placed[0], placed[1])


def solution(mesh):
    placed = (
        P(None, ("comp", "tile")),
        P(None, ("comp", "tile")),
        P(None, ("comp", "tile")),
        P(("comp", "tile")),
        P(None, None, ("comp", "tile")),
        P(("comp", "tile")),
        P(("comp", "tile")),
        P(("comp", "tile")),
        P(None, ("comp", "tile")),
    )
    return jax.shard_map(
        local,
        mesh=mesh,
        in_specs=placed,
        out_specs=(
            P(None, ("comp", "tile")),
            P(None, ("comp", "tile")),
            P(None, None, ("comp", "tile")),
            P(("comp", "tile")),
            P(("comp", "tile")),
        ),
        check_vma=False,
    )
```

profile of v0, /device:TPU:0, one launch (start us, length us, event | category | flops | bytes accessed | tf_op | source)
XLA Modules:
  0.0 319.3 jit_solution(17035251949827151419)
XLA Ops:
  0.6 2.7 fusion.41
  3.3 2.3 fusion.40
  6.7 5.0 %sort.32 = (s32[2048]{0:T(1024)}, s32[2048]{0:T(1024)S(1)}) sort(s32[2048]{0:T(1024)S(1)} %add_select_fusion, s32[2048]{0:T(1024)S(1)} %iota.53), dimensions={0}, to_apply=%region_1.2 | sort | flops 22528 | bytes 32768 | tf_op jit(solution)/shard_map/jit(argsort)/sort | solution.py:126
  12.4 5.5 %gather_fusion = f32[2048,2]{1,0:T(8,128)S(1)} fusion(f32[2,2048]{0,1:T(8,128)S(1)} %copy.30, s32[2048]{0:T(1024)S(1)} %get-tuple-element.770), kind=kCustom, calls=%fused_computation | custom fusion | bytes 40960 | tf_op jit(solution)/shard_map/gather | solution.py:129
  19.0 7.3 %all-to-all-start = ((f32[32,1,128]{2,1,0:T(1,128)}), f32[32,1,128]{2,1,0:T(1,128)S(1)}, u32[]{:S(2)}, u32[]{:S(2)}) async-start(f32[32,1,128]{2,1,0:T(1,128)} %reshape.245), calls=%async_computation | async-start | bytes 32768 | tf_op jit(solution)/shard_map/all_to_all | solution.py:130
  26.3 2.5 fusion.39
  30.5 3.6 %collective-permute-start.1 = (f32[29,36,64]{2,0,1:T(8,128)}, f32[29,36,64]{2,0,1:T(8,128)S(1)}, u32[]{:S(2)}, u32[]{:S(2)}) collective-permute-start(f32[29,36,64]{2,0,1:T(8,128)} %get-tuple-element.708), channel_id=1, source_target_pairs={{1,0},{2,1},{3,2},{4,3},{5,4},{6,5},{7,6},{8,7},{9,8},{10,9},{11,1... | collective-permute-start | bytes 801800 | tf_op jit(solution)/shard_map/ppermute | solution.py:20
  38.1 5.7 %sort.31 = (s32[2048]{0:T(1024)}, s32[2048]{0:T(1024)S(1)}) sort(s32[2048]{0:T(1024)} %param.17, s32[2048]{0:T(1024)S(1)} %iota.52), dimensions={0}, to_apply=%region_0.1 | sort | flops 22528 | bytes 32768 | tf_op jit(solution)/shard_map/jit(argsort)/sort | solution.py:127
  54.1 6.2 %scatter_custom_fusion = f32[2,2048]{0,1:T(8,128)S(1)} fusion(s32[2048]{0:T(1024)} %get-tuple-element.768, f32[2048,2]{1,0:T(8,128)S(1)} %copy.33, f32[]{:T(128)} %constant.208.clone.1), kind=kCustom, calls=%fused_computation.52 | custom fusion | bytes 16896 | tf_op jit(solution)/shard_map/scatter | solution.py:134
  61.8 12.7 %concatenate.3 = f32[29,36,2176]{2,0,1:T(8,128)} concatenate(f32[29,36,64]{2,0,1:T(8,128)S(1)} %collective-permute-done, f32[29,36,2048]{2,0,1:T(8,128)} %param.15, f32[29,36,64]{2,0,1:T(8,128)S(1)} %collective-permute-done.1), dimensions={2} | concatenate | bytes 18173952 | tf_op jit(solution)/shard_map/concatenate | solution.py:16
  74.5 13.0 %copy.29 = f32[29,36,2176]{2,1,0:T(8,128)} copy(f32[29,36,2176]{2,0,1:T(8,128)} %concatenate.3) | data formatting | bytes 18173952 | tf_op jit(solution)/shard_map/concatenate | solution.py:16
  87.5 10.0 %reshape.182 = f32[1044,2176]{1,0:T(8,128)} reshape(f32[29,36,2176]{2,1,0:T(8,128)} %copy.29) | data formatting | bytes 18173952 | tf_op jit(solution)/shard_map/reshape | solution.py:58
  97.5 4.4 %broadcast_in_dim.88 = f32[1044,2048]{1,0:T(8,128)} broadcast(f32[]{:T(128)} %constant.208.clone.1), dimensions={} | broadcast | bytes 8552452 | tf_op jit(solution)/shard_map/broadcast_in_dim | solution.py:110
  102.3 171.7 %while.22 = (s32[]{:T(128)}, f32[1044,2048]{1,0:T(8,128)}, f32[2048]{0:T(1024)S(1)}, f32[2048]{0:T(1024)S(1)}, f32[2048]{0:T(1024)}, /*index=5*/f32[1044,2176]{1...) while((s32[]{:T(128)}, f32[1044,2048]{1,0:T(8,128)}, ...), condition=%wide.region_6.7_spmd.clone.clone.clone, body=%wide.region_3.6_spmd.clone.clone.clone.sunk | while | flops 1646759424 | bytes 7693664 | solution.py:114
  103.0 2.3 fusion.47
  107.2 3.3 %multiply_reduce_fusion.5 = (f32[128]{0:T(128)S(1)}, f32[128]{0:T(128)S(1)}, f32[1044,128]{1,0:T(8,128)S(1)}) fusion(f32[1044]{0:T(1024)S(1)} %reshape.250, f32[128]{0:T(128)S(1)} %get-tuple-element.879, f32[1044]{0:T(1024)S(1)} %mul.1863, f32[128]{0:T(128)S(1)} %get-tuple-element.880, f32[1044]{0:T(1024)S(1)} %mul.1865, ...), kind=kLoop, calls=%fused_computation.23.clone.1 | loop fusion | flops 2672384 | bytes 3237388 | tf_op jit(solution)/shard_map/while/body/eval_jaxpr/reduce_sum | solution.py:100
  113.8 2.3 fusion.47
  117.9 3.3 %multiply_reduce_fusion.5 = (f32[128]{0:T(128)S(1)}, f32[128]{0:T(128)S(1)}, f32[1044,128]{1,0:T(8,128)S(1)}) fusion(f32[1044]{0:T(1024)S(1)} %reshape.250, f32[128]{0:T(128)S(1)} %get-tuple-element.879, f32[1044]{0:T(1024)S(1)} %mul.1863, f32[128]{0:T(128)S(1)} %get-tuple-element.880, f32[1044]{0:T(1024)S(1)} %mul.1865, ...), kind=kLoop, calls=%fused_computation.23.clone.1 | loop fusion | flops 2672384 | bytes 3237388 | tf_op jit(solution)/shard_map/while/body/eval_jaxpr/reduce_sum | solution.py:100
  124.5 2.3 fusion.47
  128.6 3.3 %multiply_reduce_fusion.5 = (f32[128]{0:T(128)S(1)}, f32[128]{0:T(128)S(1)}, f32[1044,128]{1,0:T(8,128)S(1)}) fusion(f32[1044]{0:T(1024)S(1)} %reshape.250, f32[128]{0:T(128)S(1)} %get-tuple-element.879, f32[1044]{0:T(1024)S(1)} %mul.1863, f32[128]{0:T(128)S(1)} %get-tuple-element.880, f32[1044]{0:T(1024)S(1)} %mul.1865, ...), kind=kLoop, calls=%fused_computation.23.clone.1 | loop fusion | flops 2672384 | bytes 3237388 | tf_op jit(solution)/shard_map/while/body/eval_jaxpr/reduce_sum | solution.py:100
  135.2 2.3 fusion.47
  139.4 3.3 %multiply_reduce_fusion.5 = (f32[128]{0:T(128)S(1)}, f32[128]{0:T(128)S(1)}, f32[1044,128]{1,0:T(8,128)S(1)}) fusion(f32[1044]{0:T(1024)S(1)} %reshape.250, f32[128]{0:T(128)S(1)} %get-tuple-element.879, f32[1044]{0:T(1024)S(1)} %mul.1863, f32[128]{0:T(128)S(1)} %get-tuple-element.880, f32[1044]{0:T(1024)S(1)} %mul.1865, ...), kind=kLoop, calls=%fused_computation.23.clone.1 | loop fusion | flops 2672384 | bytes 3237388 | tf_op jit(solution)/shard_map/while/body/eval_jaxpr/reduce_sum | solution.py:100
  150.1 3.3 %multiply_reduce_fusion.5 = (f32[128]{0:T(128)S(1)}, f32[128]{0:T(128)S(1)}, f32[1044,128]{1,0:T(8,128)S(1)}) fusion(f32[1044]{0:T(1024)S(1)} %reshape.250, f32[128]{0:T(128)S(1)} %get-tuple-element.879, f32[1044]{0:T(1024)S(1)} %mul.1863, f32[128]{0:T(128)S(1)} %get-tuple-element.880, f32[1044]{0:T(1024)S(1)} %mul.1865, ...), kind=kLoop, calls=%fused_computation.23.clone.1 | loop fusion | flops 2672384 | bytes 3237388 | tf_op jit(solution)/shard_map/while/body/eval_jaxpr/reduce_sum | solution.py:100
  160.8 3.3 %multiply_reduce_fusion.5 = (f32[128]{0:T(128)S(1)}, f32[128]{0:T(128)S(1)}, f32[1044,128]{1,0:T(8,128)S(1)}) fusion(f32[1044]{0:T(1024)S(1)} %reshape.250, f32[128]{0:T(128)S(1)} %get-tuple-element.879, f32[1044]{0:T(1024)S(1)} %mul.1863, f32[128]{0:T(128)S(1)} %get-tuple-element.880, f32[1044]{0:T(1024)S(1)} %mul.1865, ...), kind=kLoop, calls=%fused_computation.23.clone.1 | loop fusion | flops 2672384 | bytes 3237388 | tf_op jit(solution)/shard_map/while/body/eval_jaxpr/reduce_sum | solution.py:100
  167.4 2.3 fusion.47
  171.6 3.3 %multiply_reduce_fusion.5 = (f32[128]{0:T(128)S(1)}, f32[128]{0:T(128)S(1)}, f32[1044,128]{1,0:T(8,128)S(1)}) fusion(f32[1044]{0:T(1024)S(1)} %reshape.250, f32[128]{0:T(128)S(1)} %get-tuple-element.879, f32[1044]{0:T(1024)S(1)} %mul.1863, f32[128]{0:T(128)S(1)} %get-tuple-element.880, f32[1044]{0:T(1024)S(1)} %mul.1865, ...), kind=kLoop, calls=%fused_computation.23.clone.1 | loop fusion | flops 2672384 | bytes 3237388 | tf_op jit(solution)/shard_map/while/body/eval_jaxpr/reduce_sum | solution.py:100
  178.2 2.3 fusion.47
  182.3 3.3 %multiply_reduce_fusion.5 = (f32[128]{0:T(128)S(1)}, f32[128]{0:T(128)S(1)}, f32[1044,128]{1,0:T(8,128)S(1)}) fusion(f32[1044]{0:T(1024)S(1)} %reshape.250, f32[128]{0:T(128)S(1)} %get-tuple-element.879, f32[1044]{0:T(1024)S(1)} %mul.1863, f32[128]{0:T(128)S(1)} %get-tuple-element.880, f32[1044]{0:T(1024)S(1)} %mul.1865, ...), kind=kLoop, calls=%fused_computation.23.clone.1 | loop fusion | flops 2672384 | bytes 3237388 | tf_op jit(solution)/shard_map/while/body/eval_jaxpr/reduce_sum | solution.py:100
  188.9 2.3 fusion.47
  193.1 3.3 %multiply_reduce_fusion.5 = (f32[128]{0:T(128)S(1)}, f32[128]{0:T(128)S(1)}, f32[1044,128]{1,0:T(8,128)S(1)}) fusion(f32[1044]{0:T(1024)S(1)} %reshape.250, f32[128]{0:T(128)S(1)} %get-tuple-element.879, f32[1044]{0:T(1024)S(1)} %mul.1863, f32[128]{0:T(128)S(1)} %get-tuple-element.880, f32[1044]{0:T(1024)S(1)} %mul.1865, ...), kind=kLoop, calls=%fused_computation.23.clone.1 | loop fusion | flops 2672384 | bytes 3237388 | tf_op jit(solution)/shard_map/while/body/eval_jaxpr/reduce_sum | solution.py:100
  199.6 2.3 fusion.47
  203.8 3.3 %multiply_reduce_fusion.5 = (f32[128]{0:T(128)S(1)}, f32[128]{0:T(128)S(1)}, f32[1044,128]{1,0:T(8,128)S(1)}) fusion(f32[1044]{0:T(1024)S(1)} %reshape.250, f32[128]{0:T(128)S(1)} %get-tuple-element.879, f32[1044]{0:T(1024)S(1)} %mul.1863, f32[128]{0:T(128)S(1)} %get-tuple-element.880, f32[1044]{0:T(1024)S(1)} %mul.1865, ...), kind=kLoop, calls=%fused_computation.23.clone.1 | loop fusion | flops 2672384 | bytes 3237388 | tf_op jit(solution)/shard_map/while/body/eval_jaxpr/reduce_sum | solution.py:100
  210.4 2.3 fusion.47
  214.5 3.3 %multiply_reduce_fusion.5 = (f32[128]{0:T(128)S(1)}, f32[128]{0:T(128)S(1)}, f32[1044,128]{1,0:T(8,128)S(1)}) fusion(f32[1044]{0:T(1024)S(1)} %reshape.250, f32[128]{0:T(128)S(1)} %get-tuple-element.879, f32[1044]{0:T(1024)S(1)} %mul.1863, f32[128]{0:T(128)S(1)} %get-tuple-element.880, f32[1044]{0:T(1024)S(1)} %mul.1865, ...), kind=kLoop, calls=%fused_computation.23.clone.1 | loop fusion | flops 2672384 | bytes 3237388 | tf_op jit(solution)/shard_map/while/body/eval_jaxpr/reduce_sum | solution.py:100
  221.1 2.3 fusion.47
  225.3 3.3 %multiply_reduce_fusion.5 = (f32[128]{0:T(128)S(1)}, f32[128]{0:T(128)S(1)}, f32[1044,128]{1,0:T(8,128)S(1)}) fusion(f32[1044]{0:T(1024)S(1)} %reshape.250, f32[128]{0:T(128)S(1)} %get-tuple-element.879, f32[1044]{0:T(1024)S(1)} %mul.1863, f32[128]{0:T(128)S(1)} %get-tuple-element.880, f32[1044]{0:T(1024)S(1)} %mul.1865, ...), kind=kLoop, calls=%fused_computation.23.clone.1 | loop fusion | flops 2672384 | bytes 3237388 | tf_op jit(solution)/shard_map/while/body/eval_jaxpr/reduce_sum | solution.py:100
  231.8 2.3 fusion.47
  236.0 3.3 %multiply_reduce_fusion.5 = (f32[128]{0:T(128)S(1)}, f32[128]{0:T(128)S(1)}, f32[1044,128]{1,0:T(8,128)S(1)}) fusion(f32[1044]{0:T(1024)S(1)} %reshape.250, f32[128]{0:T(128)S(1)} %get-tuple-element.879, f32[1044]{0:T(1024)S(1)} %mul.1863, f32[128]{0:T(128)S(1)} %get-tuple-element.880, f32[1044]{0:T(1024)S(1)} %mul.1865, ...), kind=kLoop, calls=%fused_computation.23.clone.1 | loop fusion | flops 2672384 | bytes 3237388 | tf_op jit(solution)/shard_map/while/body/eval_jaxpr/reduce_sum | solution.py:100
  242.5 2.3 fusion.47
  246.7 3.3 %multiply_reduce_fusion.5 = (f32[128]{0:T(128)S(1)}, f32[128]{0:T(128)S(1)}, f32[1044,128]{1,0:T(8,128)S(1)}) fusion(f32[1044]{0:T(1024)S(1)} %reshape.250, f32[128]{0:T(128)S(1)} %get-tuple-element.879, f32[1044]{0:T(1024)S(1)} %mul.1863, f32[128]{0:T(128)S(1)} %get-tuple-element.880, f32[1044]{0:T(1024)S(1)} %mul.1865, ...), kind=kLoop, calls=%fused_computation.23.clone.1 | loop fusion | flops 2672384 | bytes 3237388 | tf_op jit(solution)/shard_map/while/body/eval_jaxpr/reduce_sum | solution.py:100
  257.4 3.3 %multiply_reduce_fusion.5 = (f32[128]{0:T(128)S(1)}, f32[128]{0:T(128)S(1)}, f32[1044,128]{1,0:T(8,128)S(1)}) fusion(f32[1044]{0:T(1024)S(1)} %reshape.250, f32[128]{0:T(128)S(1)} %get-tuple-element.879, f32[1044]{0:T(1024)S(1)} %mul.1863, f32[128]{0:T(128)S(1)} %get-tuple-element.880, f32[1044]{0:T(1024)S(1)} %mul.1865, ...), kind=kLoop, calls=%fused_computation.23.clone.1 | loop fusion | flops 2672384 | bytes 3237388 | tf_op jit(solution)/shard_map/while/body/eval_jaxpr/reduce_sum | solution.py:100
  264.0 2.3 fusion.47
  268.2 3.3 %multiply_reduce_fusion.5 = (f32[128]{0:T(128)S(1)}, f32[128]{0:T(128)S(1)}, f32[1044,128]{1,0:T(8,128)S(1)}) fusion(f32[1044]{0:T(1024)S(1)} %reshape.250, f32[128]{0:T(128)S(1)} %get-tuple-element.879, f32[1044]{0:T(1024)S(1)} %mul.1863, f32[128]{0:T(128)S(1)} %get-tuple-element.880, f32[1044]{0:T(1024)S(1)} %mul.1865, ...), kind=kLoop, calls=%fused_computation.23.clone.1 | loop fusion | flops 2672384 | bytes 3237388 | tf_op jit(solution)/shard_map/while/body/eval_jaxpr/reduce_sum | solution.py:100
  274.4 5.5 %gather_fusion.1 = f32[2048,2]{1,0:T(8,128)S(1)} fusion(f32[2,2048]{0,1:T(8,128)S(1)} %copy.34, s32[2048]{0:T(1024)S(1)} %copy-done.29), kind=kCustom, calls=%fused_computation.1 | custom fusion | bytes 40960 | tf_op jit(solution)/shard_map/gather | solution.py:136
  281.0 2.8 all-to-all-start.1
  288.4 9.7 %reshape.185 = f32[29,36,2048]{2,1,0:T(8,128)} reshape(f32[1044,2048]{1,0:T(8,128)} %get-tuple-element.403) | data formatting | bytes 17104896 | tf_op jit(solution)/shard_map/reshape | solution.py:115
  298.1 12.4 %copy.38 = f32[29,36,2048]{2,0,1:T(8,128)} copy(f32[29,36,2048]{2,1,0:T(8,128)} %reshape.185) | data formatting | bytes 17104896
  311.8 6.0 %scatter_custom_fusion.1 = f32[2,2048]{0,1:T(8,128)S(1)} fusion(s32[2048]{0:T(1024)} %get-tuple-element.769, f32[2048,2]{1,0:T(8,128)S(1)} %copy.37, f32[]{:T(128)} %constant.208.clone.1), kind=kCustom, calls=%fused_computation.50 | custom fusion | bytes 16896 | tf_op jit(solution)/shard_map/scatter | solution.py:138
  (442 shorter events, 117.0 us)
Async XLA Ops:
  19.0 33.4 %all-to-all-start = ((f32[32,1,128]{2,1,0:T(1,128)}), f32[32,1,128]{2,1,0:T(1,128)S(1)}, u32[]{:S(2)}, u32[]{:S(2)}) async-start(f32[32,1,128]{2,1,0:T(1,128)} %reshape.245), calls=%async_computation | async-start | bytes 32768 | tf_op jit(solution)/shard_map/all_to_all | solution.py:130
  28.7 33.1 %collective-permute-start = (f32[29,36,64]{2,0,1:T(8,128)}, f32[29,36,64]{2,0,1:T(8,128)S(1)}, u32[]{:S(2)}, u32[]{:S(2)}) collective-permute-start(f32[29,36,64]{2,0,1:T(8,128)} %get-tuple-element.709), channel_id=1, source_target_pairs={{0,1},{1,2},{2,3},{3,4},{4,5},{5,6},{6,7},{7,8},{8,9},{9,10},{10,1... | collective-permute-start | bytes 801800 | tf_op jit(solution)/shard_map/ppermute | solution.py:18
  30.5 31.3 %collective-permute-start.1 = (f32[29,36,64]{2,0,1:T(8,128)}, f32[29,36,64]{2,0,1:T(8,128)S(1)}, u32[]{:S(2)}, u32[]{:S(2)}) collective-permute-start(f32[29,36,64]{2,0,1:T(8,128)} %get-tuple-element.708), channel_id=1, source_target_pairs={{1,0},{2,1},{3,2},{4,3},{5,4},{6,5},{7,6},{8,7},{9,8},{10,9},{11,1... | collective-permute-start | bytes 801800 | tf_op jit(solution)/shard_map/ppermute | solution.py:20
  35.8 9.8 %copy-start.30 = (f32[29]{0:T(128)}, f32[29]{0:T(128)S(1)}, u32[]{:S(2)}) copy-start(f32[29]{0:T(128)S(1)} %power_multiply_fusion) | copy-start | bytes 352
  97.5 4.5 %copy-start.31 = (f32[29]{0:T(128)S(1)}, f32[29]{0:T(128)}, u32[]{:S(2)}) copy-start(f32[29]{0:T(128)} %copy-done.30) | copy-start | bytes 352
  97.5 4.5 %copy-start.32 = (f32[29]{0:T(128)S(1)}, f32[29]{0:T(128)}, u32[]{:S(2)}) copy-start(f32[29]{0:T(128)} %get-tuple-element.908) | copy-start | bytes 352
  97.5 4.5 %copy-start.33 = (f32[29]{0:T(128)S(1)}, f32[29]{0:T(128)}, u32[]{:S(2)}) copy-start(f32[29]{0:T(128)} %get-tuple-element.905) | copy-start | bytes 352
  97.5 4.5 %copy-start.34 = (f32[36]{0:T(128)S(1)}, f32[36]{0:T(128)}, u32[]{:S(2)}) copy-start(f32[36]{0:T(128)} %get-tuple-element.907) | copy-start | bytes 436
  97.5 4.5 %copy-start.35 = (f32[36]{0:T(128)S(1)}, f32[36]{0:T(128)}, u32[]{:S(2)}) copy-start(f32[36]{0:T(128)} %get-tuple-element.906) | copy-start | bytes 436
  102.0 172.4 %copy-start.29 = (s32[2048]{0:T(1024)S(1)}, s32[2048]{0:T(1024)}, u32[]{:S(2)}) copy-start(s32[2048]{0:T(1024)} %get-tuple-element.767) | copy-start | bytes 24580
  102.0 181.8 %copy-start = (f32[2048]{0:T(1024)S(1)}, f32[2048]{0:T(1024)}, u32[]{:S(2)}) copy-start(f32[2048]{0:T(1024)} %param.14) | copy-start | bytes 24580
  102.0 181.8 %copy-start.1 = (f32[2048]{0:T(1024)S(1)}, f32[2048]{0:T(1024)}, u32[]{:S(2)}) copy-start(f32[2048]{0:T(1024)} %get-tuple-element.695) | copy-start | bytes 24580
  102.0 181.8 %copy-start.2 = (f32[2048]{0:T(1024)S(1)}, f32[2048]{0:T(1024)}, u32[]{:S(2)}) copy-start(f32[2048]{0:T(1024)} %get-tuple-element.696) | copy-start | bytes 24580
  102.0 181.8 %copy-start.3 = (f32[2048]{0:T(1024)S(1)}, f32[2048]{0:T(1024)}, u32[]{:S(2)}) copy-start(f32[2048]{0:T(1024)} %get-tuple-element.697) | copy-start | bytes 24580
  102.0 181.8 %copy-start.4 = (f32[2048]{0:T(1024)S(1)}, f32[2048]{0:T(1024)}, u32[]{:S(2)}) copy-start(f32[2048]{0:T(1024)} %get-tuple-element.698) | copy-start | bytes 24580
  102.0 181.8 %copy-start.5 = (f32[2048]{0:T(1024)S(1)}, f32[2048]{0:T(1024)}, u32[]{:S(2)}) copy-start(f32[2048]{0:T(1024)} %get-tuple-element.699) | copy-start | bytes 24580
  102.1 181.8 %copy-start.6 = (f32[2048]{0:T(1024)S(1)}, f32[2048]{0:T(1024)}, u32[]{:S(2)}) copy-start(f32[2048]{0:T(1024)} %get-tuple-element.700) | copy-start | bytes 24580
  102.1 181.8 %copy-start.7 = (f32[2048]{0:T(1024)S(1)}, f32[2048]{0:T(1024)}, u32[]{:S(2)}) copy-start(f32[2048]{0:T(1024)} %get-tuple-element.701) | copy-start | bytes 24580
  102.1 181.8 %copy-start.8 = (f32[2048]{0:T(1024)S(1)}, f32[2048]{0:T(1024)}, u32[]{:S(2)}) copy-start(f32[2048]{0:T(1024)} %get-tuple-element.629) | copy-start | bytes 24580
  102.1 181.9 %copy-start.9 = (f32[2048]{0:T(1024)S(1)}, f32[2048]{0:T(1024)}, u32[]{:S(2)}) copy-start(f32[2048]{0:T(1024)} %get-tuple-element.609) | copy-start | bytes 24580
  102.1 181.9 %copy-start.10 = (f32[2048]{0:T(1024)S(1)}, f32[2048]{0:T(1024)}, u32[]{:S(2)}) copy-start(f32[2048]{0:T(1024)} %get-tuple-element.610) | copy-start | bytes 24580
  102.1 181.9 %copy-start.11 = (f32[2048]{0:T(1024)S(1)}, f32[2048]{0:T(1024)}, u32[]{:S(2)}) copy-start(f32[2048]{0:T(1024)} %get-tuple-element.611) | copy-start | bytes 24580
  102.1 181.9 %copy-start.12 = (f32[2048]{0:T(1024)S(1)}, f32[2048]{0:T(1024)}, u32[]{:S(2)}) copy-start(f32[2048]{0:T(1024)} %get-tuple-element.612) | copy-start | bytes 24580
  102.1 181.9 %copy-start.13 = (f32[2048]{0:T(1024)S(1)}, f32[2048]{0:T(1024)}, u32[]{:S(2)}) copy-start(f32[2048]{0:T(1024)} %get-tuple-element.613) | copy-start | bytes 24580
  102.1 181.9 %copy-start.14 = (f32[2048]{0:T(1024)S(1)}, f32[2048]{0:T(1024)}, u32[]{:S(2)}) copy-start(f32[2048]{0:T(1024)} %get-tuple-element.614) | copy-start | bytes 24580
  102.1 181.9 %copy-start.15 = (f32[2048]{0:T(1024)S(1)}, f32[2048]{0:T(1024)}, u32[]{:S(2)}) copy-start(f32[2048]{0:T(1024)} %get-tuple-element.615) | copy-start | bytes 24580
  102.2 181.9 %copy-start.16 = (f32[2048]{0:T(1024)S(1)}, f32[2048]{0:T(1024)}, u32[]{:S(2)}) copy-start(f32[2048]{0:T(1024)} %get-tuple-element.616) | copy-start | bytes 24580
  102.2 181.9 %copy-start.17 = (f32[2048]{0:T(1024)S(1)}, f32[2048]{0:T(1024)}, u32[]{:S(2)}) copy-start(f32[2048]{0:T(1024)} %get-tuple-element.617) | copy-start | bytes 24580
  102.2 181.9 %copy-start.18 = (f32[2048]{0:T(1024)S(1)}, f32[2048]{0:T(1024)}, u32[]{:S(2)}) copy-start(f32[2048]{0:T(1024)} %get-tuple-element.618) | copy-start | bytes 24580
  102.2 181.9 %copy-start.19 = (f32[2048]{0:T(1024)S(1)}, f32[2048]{0:T(1024)}, u32[]{:S(2)}) copy-start(f32[2048]{0:T(1024)} %get-tuple-element.619) | copy-start | bytes 24580
  102.2 181.9 %copy-start.20 = (f32[2048]{0:T(1024)S(1)}, f32[2048]{0:T(1024)}, u32[]{:S(2)}) copy-start(f32[2048]{0:T(1024)} %get-tuple-element.620) | copy-start | bytes 24580
  102.2 181.9 %copy-start.21 = (f32[2048]{0:T(1024)S(1)}, f32[2048]{0:T(1024)}, u32[]{:S(2)}) copy-start(f32[2048]{0:T(1024)} %get-tuple-element.621) | copy-start | bytes 24580
  102.2 181.9 %copy-start.22 = (f32[2048]{0:T(1024)S(1)}, f32[2048]{0:T(1024)}, u32[]{:S(2)}) copy-start(f32[2048]{0:T(1024)} %get-tuple-element.622) | copy-start | bytes 24580
  102.2 181.9 %copy-start.23 = (f32[2048]{0:T(1024)S(1)}, f32[2048]{0:T(1024)}, u32[]{:S(2)}) copy-start(f32[2048]{0:T(1024)} %get-tuple-element.623) | copy-start | bytes 24580
  102.2 181.9 %copy-start.24 = (f32[2048]{0:T(1024)S(1)}, f32[2048]{0:T(1024)}, u32[]{:S(2)}) copy-start(f32[2048]{0:T(1024)} %get-tuple-element.624) | copy-start | bytes 24580
  102.2 181.9 %copy-start.25 = (f32[2048]{0:T(1024)S(1)}, f32[2048]{0:T(1024)}, u32[]{:S(2)}) copy-start(f32[2048]{0:T(1024)} %get-tuple-element.625) | copy-start | bytes 24580
  102.3 181.9 %copy-start.26 = (f32[2048]{0:T(1024)S(1)}, f32[2048]{0:T(1024)}, u32[]{:S(2)}) copy-start(f32[2048]{0:T(1024)} %get-tuple-element.626) | copy-start | bytes 24580
  102.3 181.9 %copy-start.27 = (f32[2048]{0:T(1024)S(1)}, f32[2048]{0:T(1024)}, u32[]{:S(2)}) copy-start(f32[2048]{0:T(1024)} %get-tuple-element.627) | copy-start | bytes 24580
  102.3 181.9 %copy-start.28 = (f32[2048]{0:T(1024)S(1)}, f32[2048]{0:T(1024)}, u32[]{:S(2)}) copy-start(f32[2048]{0:T(1024)} %get-tuple-element.628) | copy-start | bytes 24580
  281.0 29.6 %all-to-all-start.1 = ((f32[32,1,128]{2,1,0:T(1,128)}), f32[32,1,128]{2,1,0:T(1,128)S(1)}, u32[]{:S(2)}, u32[]{:S(2)}) async-start(f32[32,1,128]{2,1,0:T(1,128)} %reshape.247), calls=%async_computation.1 | async-start | bytes 32768 | tf_op jit(solution)/shard_map/all_to_all | solution.py:137
where the time goes:
time: 324 us; the launch traced here: 319 us
  other arithmetic  140 us (43%)
  local copies, waits for them, and re-layouts  124 us (38%)
  matrix products  36.7 us (11%)
  starting transfers between devices  15.4 us (5%)
    reduce_sum x16, other arithmetic, advance(): tau_wave = fmask * jnp.mean(sigma * gamma * moved, axis=0)  52.1 us
    dot_general x16, matrix products, advance(): jnp.dot(window, table, precision=lax.Precision.HIGHEST, preferred_element...  36.7 us
    dynamic_update_slice x16, other arithmetic, advance(): spec_out = lax.dynamic_update_slice_in_dim(spec_out, new_spec, start, 1)  27.2 us
    concatenate x2, local copies, waits for them, and re-layouts, extended(): jnp.concatenate([lax.ppermute(tail, axis, [(i, (i + 1) % count) for i in...  25.7 us
    dynamic_update_slice x16, other arithmetic, advance(): tau_out = lax.dynamic_update_slice_in_dim(tau_out, ustar * ustar, start, 0)  14.3 us
    unnamed x77, local copies, waits for them, and re-layouts  14.2 us
    mul x16, other arithmetic, advance(): ustar0 = 0.035 * speed  12.7 us
    eq x16, other arithmetic, advance(): positions == nearest[None]  11 us
  transfers between devices with their start and end apart: 4, of which 0 were waited for; matrix products, arithmetic and copies ran while one was open for 18% of the time, Pallas kernels for 0%

commit v1 on v0

v1 whole, which is shorter than its diff:
```python
import math

import jax
import jax.numpy as jnp
import numpy as np
from jax import lax
from jax.experimental import pallas as pl
from jax.experimental.pallas import tpu as pltpu
from jax.sharding import PartitionSpec as P

HALO = 64
LANES = 128
AXES = ("comp", "tile")


def split3(value):
    first = value.astype(jnp.bfloat16)
    rest = value - first.astype(jnp.float32)
    second = rest.astype(jnp.bfloat16)
    third = (rest - second.astype(jnp.float32)).astype(jnp.bfloat16)
    return [first, second, third]


def nt_dot(a, b):
    return lax.dot_general(
        a, b, (((1,), (1,)), ((), ())), preferred_element_type=jnp.float32
    )


def one_hot(rows, index):
    iota = lax.broadcasted_iota(jnp.int32, (rows, index.shape[1]), 0)
    return jnp.where(iota == index, 1.0, 0.0)


def fill_outbox(target, values, outbox, columns):
    devices = outbox.shape[0]
    blocks = columns // LANES
    shift = int(math.log2(columns))
    hots = []
    for b in range(blocks):
        peer = lax.shift_right_logical(target[b : b + 1, :], shift)
        hots.append(one_hot(devices, peer))
    stacked = jnp.concatenate(hots, axis=0).astype(jnp.bfloat16)
    upper = jnp.where(
        lax.broadcasted_iota(jnp.int32, (LANES, LANES), 0)
        <= lax.broadcasted_iota(jnp.int32, (LANES, LANES), 1),
        1.0,
        0.0,
    ).astype(jnp.bfloat16)
    counts = jnp.dot(stacked, upper, preferred_element_type=jnp.float32)
    before = jnp.zeros((devices, 1), jnp.float32)
    total = None
    for b in range(blocks):
        hot = hots[b]
        count = counts[b * devices : (b + 1) * devices]
        rank = jnp.sum(hot * (count + before), axis=0, keepdims=True) - 1.0
        before = before + count[:, LANES - 1 :]
        place = jnp.bitwise_and(target[b : b + 1, :], columns - 1)
        high = lax.shift_right_logical(place, 7).astype(jnp.float32)
        low = jnp.bitwise_and(place, LANES - 1).astype(jnp.float32)
        rows = []
        for value in values:
            rows.extend(split3(hot * value[b : b + 1, :]))
        rows.append((hot * (high + 1.0)).astype(jnp.bfloat16))
        rows.append((hot * low).astype(jnp.bfloat16))
        ranks = one_hot(LANES, rank.astype(jnp.int32)).astype(jnp.bfloat16)
        part = nt_dot(jnp.concatenate(rows, axis=0), ranks)
        total = part if total is None else total + part
    piece = [total[i * devices : (i + 1) * devices] for i in range(8)]
    outbox[:, 0, :] = piece[0] + piece[1] + piece[2]
    outbox[:, 1, :] = piece[3] + piece[4] + piece[5]
    outbox[:, 2, :] = (piece[6] - 1.0) * LANES + piece[7]


def empty_inbox(inbox, blocks):
    devices = inbox.shape[0]
    total = jnp.zeros((6 * blocks, LANES), jnp.float32)
    for d in range(0, devices, 2):
        lefts, rights = [], []
        for e in (d, d + 1):
            place = inbox[e, 2:3, :].astype(jnp.int32)
            high = one_hot(blocks, lax.shift_right_arithmetic(place, 7))
            low = one_hot(LANES, jnp.bitwise_and(place, LANES - 1)).astype(jnp.bfloat16)
            rows = []
            for v in range(2):
                rows.extend(split3(high * inbox[e, v : v + 1, :]))
            lefts.append(jnp.concatenate(rows, axis=0))
            rights.append(low)
        total += nt_dot(jnp.concatenate(lefts, axis=1), jnp.concatenate(rights, axis=1))
    piece = [total[i * blocks : (i + 1) * blocks] for i in range(6)]
    return piece[0] + piece[1] + piece[2], piece[3] + piece[4] + piece[5]


def pack_kernel(target, first, second, outbox):
    outbox[...] = jnp.zeros_like(outbox)
    fill_outbox(target, (first, second), outbox, first.shape[0] * LANES)


def unpack_kernel(inbox, first, second):
    first[...], second[...] = empty_inbox(inbox, first.shape[0])


def solve_kernel(u_ref, v_ref, mixing, drag, u_out, v_out):
    lev = u_ref.shape[0]
    cps = []
    for k in range(lev):
        row = slice(k, k + 1)
        diag = 1.0
        if k > 0:
            above = mixing[k - 1 : k, :]
            diag = diag + above
        if k < lev - 1:
            below = mixing[row, :]
            diag = diag + below
        if k == lev - 1:
            diag = diag + drag[...]
        if k == 0:
            inverse = 1.0 / diag
            du, dv = u_ref[row, :] * inverse, v_ref[row, :] * inverse
        else:
            inverse = 1.0 / (diag - above * cps[-1])
            du = (u_ref[row, :] + above * du) * inverse
            dv = (v_ref[row, :] + above * dv) * inverse
        u_out[row, :] = du
        v_out[row, :] = dv
        if k < lev - 1:
            cps.append(below * inverse)
            cps[-1] = -cps[-1]
    for k in range(lev - 2, -1, -1):
        row = slice(k, k + 1)
        du = u_out[row, :] - cps[k] * du
        dv = v_out[row, :] - cps[k] * dv
        u_out[row, :] = du
        v_out[row, :] = dv


def rim_kernel(first, last, head, tail):
    nfreq = first.shape[0]
    half = head.shape[0]
    for f in range(half):
        lane = lax.broadcasted_iota(jnp.int32, first.shape[1:], 1)
        g = min(f + half, nfreq - 1)
        head[f] = jnp.where(lane < HALO, first[f], pltpu.roll(first[g], HALO, 1))
        tail[f] = jnp.where(lane >= HALO, last[f], pltpu.roll(last[g], HALO, 1))


def wave_kernel(
    spectrum, before, after, nbr, mask, wind_u, wind_v, spec_out, logz, tau, pad, new, sem_in, sem_out
):
    nfreq, ndir, width = spectrum.shape
    blocks = width // LANES
    half = before.shape[0]
    freq = (np.float32(0.0418) * np.float32(1.1) ** np.arange(nfreq, dtype=np.float32)).astype(np.float64)
    courant = 0.7 * freq[0] / freq
    sigma = freq / freq[-1]
    theta = 2.0 * math.pi * (np.arange(ndir) + 0.5) / ndir
    cos, sin = np.cos(theta), np.sin(theta)
    tiles = [(d, min(8, ndir - d)) for d in range(0, ndir, 8)]
    f32 = jnp.float32

    def load(c):
        lanes = pl.ds(pl.multiple_of(c * LANES, LANES), LANES)
        padded = pl.ds(pl.multiple_of(c * LANES + LANES, LANES), LANES)
        return pltpu.make_async_copy(spectrum.at[:, :, lanes], pad.at[:, :, padded], sem_in.at[c])

    def store(c):
        lanes = pl.ds(pl.multiple_of(c * LANES, LANES), LANES)
        return pltpu.make_async_copy(new.at[:, :, lanes], spec_out.at[:, :, lanes], sem_out.at[c])

    def column(values, d, n):
        iota = lax.broadcasted_iota(jnp.int32, (n, LANES), 0)
        result = jnp.full((n, LANES), float(values[d]), f32)
        for i in range(1, n):
            result = jnp.where(iota == i, float(values[d + i]), result)
        return result

    for c in range(blocks):
        load(c).start()
    for f in range(half):
        pad[f, :, 0:LANES] = before[f]
        pad[f, :, width + LANES :] = after[f]
        if f + half < nfreq:
            pad[f + half, :, 0:LANES] = pltpu.roll(before[f], HALO, 1)
            pad[f + half, :, width + LANES :] = pltpu.roll(after[f], HALO, 1)
    load(0).wait()

    def advance(j, carry):
        @pl.when(j < blocks - 1)
        def _():
            load(j + 1).wait()

        at = pl.multiple_of(j * LANES, LANES)
        here = pl.ds(at, LANES)
        west = nbr[0:1, here] - HALO - at
        east = nbr[1:2, here] - HALO - at
        south = nbr[2:3, here] - HALO - at
        north = nbr[3:4, here] - HALO - at
        wu = wind_u[pl.ds(j, 1), :]
        wv = wind_v[pl.ds(j, 1), :]
        fm = mask[pl.ds(j, 1), :].astype(f32)

        def block(shift, f, d, n):
            return pad[f, d : d + n, pl.ds(pl.multiple_of(at + shift * LANES, LANES), LANES)]

        energy = jnp.zeros((1, LANES), f32)
        push = jnp.zeros((1, LANES), f32)
        drives = []
        for d, n in tiles:
            iota = lax.broadcasted_iota(jnp.int32, (n, LANES), 0) + d

            def way(values, low, high):
                lows = [bool(values[d + i] > 0) for i in range(n)]
                if all(lows):
                    rel, pick = jnp.broadcast_to(low, (n, LANES)), 0
                elif not any(lows):
                    rel, pick = jnp.broadcast_to(high, (n, LANES)), 2
                else:
                    edge = next(i for i in range(1, n) if lows[i] != lows[0])
                    pick = (iota < d + edge) if lows[0] else (iota >= d + edge)
                    rel = jnp.where(pick, low, high)
                own = jnp.logical_and(rel >= 0, rel < LANES)
                return own, jnp.bitwise_and(rel, LANES - 1), pick

            own_x, at_x, pick_x = way(cos, west, east)
            own_y, at_y, pick_y = way(sin, south, north)
            wide = jnp.abs(column(cos, d, n))
            tall = jnp.abs(column(sin, d, n))
            drive = 0.63 * (wu * column(cos, d, n) + wv * column(sin, d, n))
            drives.append(drive)
            total = jnp.zeros((n, LANES), f32)
            total_push = jnp.zeros((n, LANES), f32)
            for f in range(nfreq):
                cell = block(1, f, d, n)

                def upwind(own, index, pick):
                    if isinstance(pick, int):
                        other = block(pick, f, d, n)
                    else:
                        other = jnp.where(pick, block(0, f, d, n), block(2, f, d, n))
                    return jnp.where(
                        own,
                        jnp.take_along_axis(cell, index, axis=1, mode="promise_in_bounds"),
                        jnp.take_along_axis(other, index, axis=1, mode="promise_in_bounds"),
                    )

                upx = upwind(own_x, at_x, pick_x)
                upy = upwind(own_y, at_y, pick_y)
                moved = cell + float(courant[f]) * (wide * (upx - cell) + tall * (upy - cell))
                new[f, d : d + n, here] = moved
                total = total + moved
                gain = jnp.maximum(0.0, float(sigma[f] * freq[f]) * drive - float(sigma[f]))
                total_push = total_push + gain * moved
            energy = energy + jnp.sum(total, axis=0, keepdims=True)
            push = push + jnp.sum(total_push, axis=0, keepdims=True)

        energy = energy / float(nfreq * ndir)
        damp = fm * (0.5 * energy / (1.0 + energy))
        speed = jnp.maximum(jnp.sqrt(wu * wu + wv * wv), 1.0)
        ustar0 = 0.035 * speed
        tau_wave = fm * (push / float(nfreq * ndir))
        ratio = jnp.minimum(tau_wave / (ustar0 * ustar0), 0.9)
        z0 = 0.01 / jnp.sqrt(1.0 - ratio) * ustar0 * ustar0 / 9.81 + 1.5e-05
        ustar = 0.4 * speed / jnp.log(10.0 / z0)
        logz[pl.ds(j, 1), :] = jnp.log(z0)
        tau[pl.ds(j, 1), :] = ustar * ustar
        for (d, n), drive in zip(tiles, drives):
            drive = drive * fm
            fmb = jnp.broadcast_to(fm, (n, LANES))
            dampb = jnp.broadcast_to(damp, (n, LANES))
            for f in range(nfreq):
                gain = jnp.maximum(
                    0.0, float(0.3 * sigma[f] * freq[f]) * drive - float(0.3 * sigma[f]) * fmb
                )
                growth = fmb - float(sigma[f]) * dampb + gain
                new[f, d : d + n, here] = new[f, d : d + n, here] * growth
        store(j).start()
        return carry

    lax.fori_loop(0, blocks, advance, 0)
    for c in range(blocks):
        store(c).wait()


VMEM = pl.BlockSpec(memory_space=pltpu.VMEM)
ANY = pl.BlockSpec(memory_space=pl.ANY)
LIMIT = 48 * 1024 * 1024


def local(
    atm_u, atm_v, mixing, drag_prev, spectrum, sea_mask, wave_source, column_target, neighbours
):
    lev, columns = atm_u.shape
    nfreq, ndir, width = spectrum.shape
    devices = lax.axis_size("comp") * lax.axis_size("tile")
    blocks = columns // LANES
    half = (nfreq + 1) // 2
    f32 = jnp.float32
    params = pltpu.CompilerParams(vmem_limit_bytes=LIMIT)
    square = jax.ShapeDtypeStruct((blocks, LANES), f32)
    box = jax.ShapeDtypeStruct((devices, 8, LANES), f32)

    rim = jax.ShapeDtypeStruct((half, ndir, LANES), f32)
    edge = lambda at: pl.BlockSpec((nfreq, ndir, LANES), lambda i: (0, 0, at))
    whole = pl.BlockSpec((half, ndir, LANES), lambda i: (0, 0, 0))
    head, tail = pl.pallas_call(
        rim_kernel,
        grid=(1,),
        in_specs=[edge(0), edge(width // LANES - 1)],
        out_specs=[whole, whole],
        out_shape=[rim, rim],
        compiler_params=params,
    )(spectrum, spectrum)
    up = [(i, (i + 1) % devices) for i in range(devices)]
    before = lax.ppermute(tail, AXES, up)
    after = lax.ppermute(head, AXES, [(b, a) for a, b in up])

    def relay(target, first, second):
        outbox = pl.pallas_call(
            pack_kernel, in_specs=[VMEM] * 3, out_specs=VMEM, out_shape=box, compiler_params=params
        )(target.reshape(blocks, LANES), first, second)
        inbox = lax.all_to_all(outbox, AXES, split_axis=0, concat_axis=0, tiled=True)
        return pl.pallas_call(
            unpack_kernel, in_specs=[VMEM], out_specs=[VMEM] * 2, out_shape=[square] * 2, compiler_params=params
        )(inbox)

    wind_u, wind_v = relay(
        column_target, atm_u[-1].reshape(blocks, LANES), atm_v[-1].reshape(blocks, LANES)
    )
    slab = jax.ShapeDtypeStruct((lev, columns), f32)
    u_new, v_new = pl.pallas_call(
        solve_kernel,
        in_specs=[VMEM] * 4,
        out_specs=[VMEM] * 2,
        out_shape=[slab, slab],
        compiler_params=params,
        cost_estimate=pl.CostEstimate(flops=20 * lev * columns, bytes_accessed=20 * lev * columns, transcendentals=0),
    )(atm_u, atm_v, mixing, drag_prev.reshape(1, columns))
    spectrum_new, logz, tau = pl.pallas_call(
        wave_kernel,
        in_specs=[ANY] + [VMEM] * 6,
        out_specs=[ANY, VMEM, VMEM],
        out_shape=[jax.ShapeDtypeStruct(spectrum.shape, f32), square, square],
        scratch_shapes=[
            pltpu.VMEM((nfreq, ndir, width + 2 * LANES), f32),
            pltpu.VMEM((nfreq, ndir, width), f32),
            pltpu.SemaphoreType.DMA((blocks,)),
            pltpu.SemaphoreType.DMA((blocks,)),
        ],
        compiler_params=params,
        cost_estimate=pl.CostEstimate(
            flops=30 * spectrum.size, bytes_accessed=8 * spectrum.size, transcendentals=0
        ),
    )(spectrum, before, after, neighbours, sea_mask.reshape(blocks, LANES), wind_u, wind_v)
    rough, stress = relay(wave_source, logz, tau)
    return (u_new, v_new, spectrum_new, rough.reshape(columns), stress.reshape(columns))


def solution(mesh):
    cols, items = P(None, AXES), P(AXES)
    cube = P(None, None, AXES)
    return jax.shard_map(
        local,
        mesh=mesh,
        in_specs=(cols, cols, cols, items, cube, items, items, items, cols),
        out_specs=(cols, cols, cube, items, items),
        check_vma=False,
    )
```

time: 324 us -> 84.5 us (0.26); the launches traced: 319 us -> 84.3 us
  other arithmetic: 140 us -> 0 us
  local copies, waits for them, and re-layouts: 124 us -> 24.8 us
  matrix products: 36.7 us -> 0 us
  Pallas kernels: 0 us -> 35 us
  blocking collectives: 0 us -> 13.2 us
  starting transfers between devices: 15.4 us -> 10.4 us
    reduce_sum x16 -> x0, other arithmetic: 52.1 us -> none  [advance(): tau_wave = fmask * jnp.mean(sigma * gamma * moved, axis=0)]
    dynamic_update_slice x32 -> x0, other arithmetic: 41.5 us -> none  [the longest x16 27.2 us: advance(): spec_out = lax.dynamic_update_slice_in_dim(spec_out, new_spec, start, 1)]
    dot_general x16 -> x0, matrix products: 36.7 us -> none  [advance(): jnp.dot(window, table, precision=lax.Precision.HIGHEST, preferred_element...]
    pallas_call x0 -> x7, Pallas kernels: none -> 35 us  [the longest x1 28.7 us: local(): pl.pallas_call(wave_kernel, in_specs=[ANY] + [VMEM] * 6, out_specs=[ANY,...]
    concatenate x2 -> x0, local copies, waits for them, and re-layouts: 25.7 us -> none  [extended(): jnp.concatenate([lax.ppermute(tail, axis, [(i, (i + 1) % count) for i in...]
    reshape x8 -> x0, local copies, waits for them, and re-layouts: 21.4 us -> none  [the longest x1 10 us: wave_block(): flat = padded.reshape(rows_all, total)]
    slice x9 -> x2, local copies, waits for them, and re-layouts: 14.5 us -> 0.02 us  [the longest x1 0.01 us: local(): atm_v[-1].reshape(blocks, LANES)]
    all_to_all x0 -> x1, blocking collectives: none -> 13.2 us  [relay(): lax.all_to_all(outbox, AXES, split_axis=0, concat_axis=0, tiled=True)]
  transfers between devices with their start and end apart: 4 -> 3, of which waited for: 0 -> 0; matrix products, arithmetic and copies ran while one was open for 18% -> 15% of each run, Pallas kernels for 0% -> 3%
where the time goes in v1:
time: 84.5 us; the launch traced here: 84.3 us
  Pallas kernels  35 us (41%)
  local copies, waits for them, and re-layouts  24.8 us (29%)
  blocking collectives  13.2 us (16%)
  starting transfers between devices  10.4 us (12%)
    pallas_call x1, Pallas kernels, local(): pl.pallas_call(wave_kernel, in_specs=[ANY] + [VMEM] * 6, out_specs=[ANY,...  28.7 us
    unnamed x18, local copies, waits for them, and re-layouts  24.8 us
    all_to_all x1, blocking collectives, relay(): lax.all_to_all(outbox, AXES, split_axis=0, concat_axis=0, tiled=True)  13.2 us
    all_to_all x1, starting transfers between devices, relay(): lax.all_to_all(outbox, AXES, split_axis=0, concat_axis=0, tiled=True)  3.92 us
    ppermute x1, starting transfers between devices, local(): after = lax.ppermute(head, AXES, [(b, a) for a, b in up])  3.5 us
    ppermute x1, starting transfers between devices, local(): before = lax.ppermute(tail, AXES, up)  3 us
    pallas_call x2, Pallas kernels, relay(): pl.pallas_call(pack_kernel, in_specs=[VMEM] * 3, out_specs=VMEM, out_shap...  2.27 us
  transfers between devices with their start and end apart: 3, of which 0 were waited for; matrix products, arithmetic and copies ran while one was open for 15% of the time, Pallas kernels for 3%

profile of v1, /device:TPU:0, one launch (start us, length us, event | category | flops | bytes accessed | tf_op | source)
XLA Modules:
  0.0 84.3 jit_solution(18202591565386602683)
XLA Ops:
  0.6 12.3 %copy.16.first.last.spectrum = f32[29,36,2048]{2,1,0:T(8,128)} copy(f32[29,36,2048]{2,0,1:T(8,128)} %param.13) | data formatting | bytes 17104896 | tf_op args[4]
  13.0 0.0 copy-start
  13.0 0.0 copy-start.1
  13.0 0.0 copy-start.6
  13.0 0.0 copy-start.3
  13.0 0.0 copy-start.4
  13.0 1.5 %shard_map.129 = (f32[15,36,128]{2,1,0:T(8,128)S(1)}, f32[15,36,128]{2,1,0:T(8,128)S(1)}) custom-call(f32[29,36,2048]{2,1,0:T(8,128)} %copy.16.first.last.spectrum, f32[29,36,2048]{2,1,0:T(8,128)} %copy.16.first.last.spectrum), custom_call_target="tpu_custom_call" | custom-call | tf_op jit(solution)/shard_map/pallas_call | solution.py:305
  14.5 0.0 copy-start.7
  14.5 0.0 copy-start.2
  14.5 0.0 copy-start.5
  14.6 3.0 %collective-permute-start = (f32[15,36,128]{2,1,0:T(8,128)S(1)}, f32[15,36,128]{2,1,0:T(8,128)S(1)}, u32[]{:S(2)}, u32[]{:S(2)}) collective-permute-start(f32[15,36,128]{2,1,0:T(8,128)S(1)} %get-tuple-element.18), channel_id=1, source_target_pairs={{0,1},{1,2},{2,3},{3,4},{4,5},{5,6},{6,7},{7,8},{8,9},{9,10},{10,1... | collective-permute-start | bytes 829448 | tf_op jit(solution)/shard_map/ppermute | solution.py:314
  17.6 3.5 %collective-permute-start.1 = (f32[15,36,128]{2,1,0:T(8,128)S(1)}, f32[15,36,128]{2,1,0:T(8,128)S(1)}, u32[]{:S(2)}, u32[]{:S(2)}) collective-permute-start(f32[15,36,128]{2,1,0:T(8,128)S(1)} %get-tuple-element.19), channel_id=1, source_target_pairs={{1,0},{2,1},{3,2},{4,3},{5,4},{6,5},{7,6},{8,7},{9,8},{10,9},{11,1... | collective-permute-start | bytes 829448 | tf_op jit(solution)/shard_map/ppermute | solution.py:315
  21.1 0.0 copy-done
  21.1 0.0 copy-done.1
  21.1 0.0 copy-done.6
  21.1 0.8 shard_map.130
  21.9 13.2 %all_to_all.10.inbox = f32[32,8,128]{2,1,0:T(8,128)S(1)} all-to-all(f32[32,8,128]{2,1,0:T(8,128)S(1)} %shard_map.130), channel_id=1, replica_groups=mesh['comp'=4,'tile'=8] {'comp','tile'}, dimensions={0} | all-to-all | bytes 262144 | tf_op jit(solution)/shard_map/all_to_all | solution.py:321
  35.1 0.4 shard_map.131
  35.6 0.0 collective-permute-done.before
  35.6 0.0 collective-permute-done.1.after
  35.6 0.0 copy-done.3
  35.6 0.0 copy-done.4
  35.6 28.7 %shard_map.132 = (f32[29,36,2048]{2,1,0:T(8,128)}, f32[16,128]{1,0:T(8,128)S(1)}, f32[16,128]{1,0:T(8,128)S(1)}) custom-call(f32[29,36,2048]{2,1,0:T(8,128)} %copy.16.first.last.spectrum, f32[15,36,128]{2,1,0:T(8,128)S(1)} %collective-permute-done.before, f32[15,36,128]{2,1,0:T(8,128)S(1)} %collective-permute-done.1.after, s32[4,2048]{1,0:T(4,128)S(1)} %copy-done.3, ...), custom_call_target="tpu_custom_call" | custom-call | flops 64143360 | bytes 17104896 | tf_op jit(solution)/shard_map/pallas_call | solution.py:338
  64.3 0.0 copy-done.7
  64.3 1.5 %shard_map.133 = f32[32,8,128]{2,1,0:T(8,128)} custom-call(s32[16,128]{1,0:T(8,128)S(1)} %bitcast.13, f32[16,128]{1,0:T(8,128)S(1)} %get-tuple-element.23.first, f32[16,128]{1,0:T(8,128)S(1)} %get-tuple-element.24.second), custom_call_target="tpu_custom_call" | custom-call | tf_op jit(solution)/shard_map/pallas_call | solution.py:318
  65.8 3.9 %all-to-all-start.1 = ((f32[32,8,128]{2,1,0:T(8,128)}), f32[32,8,128]{2,1,0:T(8,128)S(1)}, u32[]{:S(2)}, u32[]{:S(2)}) async-start(f32[32,8,128]{2,1,0:T(8,128)} %shard_map.133), calls=%async_computation.1 | async-start | bytes 262144 | tf_op jit(solution)/shard_map/all_to_all | solution.py:321
  69.7 0.0 copy-done.2
  69.7 0.0 copy-done.5
  69.7 1.1 %shard_map.128 = (f32[20,2048]{1,0:T(8,128)}, f32[20,2048]{1,0:T(8,128)}) custom-call(f32[20,2048]{1,0:T(8,128)S(1)} %copy-done, f32[20,2048]{1,0:T(8,128)S(1)} %copy-done.1, f32[19,2048]{1,0:T(8,128)S(1)} %copy-done.2, f32[1,2048]{1,0:T(1,128)S(1)} %bitcast.11), custom_call_target="tpu_custom_call" | custom-call | flops 819200 | bytes 819200 | tf_op jit(solution)/shard_map/pallas_call | solution.py:330
  70.8 12.4 %copy.17 = f32[29,36,2048]{2,0,1:T(8,128)} copy(f32[29,36,2048]{2,1,0:T(8,128)} %get-tuple-element.29) | data formatting | bytes 17104896
  83.2 0.0 all-to-all-done.1.inbox
  83.2 1.0 %shard_map.134 = (f32[16,128]{1,0:T(8,128)}, f32[16,128]{1,0:T(8,128)}) custom-call(f32[32,8,128]{2,1,0:T(8,128)S(1)} %all-to-all-done.1.inbox), custom_call_target="tpu_custom_call" | custom-call | tf_op jit(solution)/shard_map/pallas_call | solution.py:322
  (2 shorter events, 0.0 us)
Async XLA Ops:
  13.0 8.1 %copy-start = (f32[20,2048]{1,0:T(8,128)S(1)}, f32[20,2048]{1,0:T(8,128)}, u32[]{:S(2)}) copy-start(f32[20,2048]{1,0:T(8,128)} %u_ref.1) | copy-start | bytes 491524
  13.0 8.1 %copy-start.1 = (f32[20,2048]{1,0:T(8,128)S(1)}, f32[20,2048]{1,0:T(8,128)}, u32[]{:S(2)}) copy-start(f32[20,2048]{1,0:T(8,128)} %v_ref.1) | copy-start | bytes 491524
  13.0 8.1 %copy-start.6 = (s32[2048]{0:T(1024)S(1)}, s32[2048]{0:T(1024)}, u32[]{:S(2)}) copy-start(s32[2048]{0:T(1024)} %param.16) | copy-start | bytes 24580
  13.0 22.6 %copy-start.3 = (s32[4,2048]{1,0:T(4,128)S(1)}, s32[4,2048]{1,0:T(4,128)}, u32[]{:S(2)}) copy-start(s32[4,2048]{1,0:T(4,128)} %nbr.1) | copy-start | bytes 98308
  13.0 22.6 %copy-start.4 = (s32[2048]{0:T(1024)S(1)}, s32[2048]{0:T(1024)}, u32[]{:S(2)}) copy-start(s32[2048]{0:T(1024)} %param.14) | copy-start | bytes 24580
  14.5 49.8 %copy-start.7 = (s32[2048]{0:T(1024)S(1)}, s32[2048]{0:T(1024)}, u32[]{:S(2)}) copy-start(s32[2048]{0:T(1024)} %param.15) | copy-start | bytes 24580
  14.5 55.1 %copy-start.2 = (f32[19,2048]{1,0:T(8,128)S(1)}, f32[19,2048]{1,0:T(8,128)}, u32[]{:S(2)}) copy-start(f32[19,2048]{1,0:T(8,128)} %mixing.1) | copy-start | bytes 466948
  14.5 55.1 %copy-start.5 = (f32[2048]{0:T(1024)S(1)}, f32[2048]{0:T(1024)}, u32[]{:S(2)}) copy-start(f32[2048]{0:T(1024)} %param.12) | copy-start | bytes 24580
  14.6 21.0 %collective-permute-start = (f32[15,36,128]{2,1,0:T(8,128)S(1)}, f32[15,36,128]{2,1,0:T(8,128)S(1)}, u32[]{:S(2)}, u32[]{:S(2)}) collective-permute-start(f32[15,36,128]{2,1,0:T(8,128)S(1)} %get-tuple-element.18), channel_id=1, source_target_pairs={{0,1},{1,2},{2,3},{3,4},{4,5},{5,6},{6,7},{7,8},{8,9},{9,10},{10,1... | collective-permute-start | bytes 829448 | tf_op jit(solution)/shard_map/ppermute | solution.py:314
  17.6 18.0 %collective-permute-start.1 = (f32[15,36,128]{2,1,0:T(8,128)S(1)}, f32[15,36,128]{2,1,0:T(8,128)S(1)}, u32[]{:S(2)}, u32[]{:S(2)}) collective-permute-start(f32[15,36,128]{2,1,0:T(8,128)S(1)} %get-tuple-element.19), channel_id=1, source_target_pairs={{1,0},{2,1},{3,2},{4,3},{5,4},{6,5},{7,6},{8,7},{9,8},{10,9},{11,1... | collective-permute-start | bytes 829448 | tf_op jit(solution)/shard_map/ppermute | solution.py:315
  65.8 17.5 %all-to-all-start.1 = ((f32[32,8,128]{2,1,0:T(8,128)}), f32[32,8,128]{2,1,0:T(8,128)S(1)}, u32[]{:S(2)}, u32[]{:S(2)}) async-start(f32[32,8,128]{2,1,0:T(8,128)} %shard_map.133), calls=%async_computation.1 | async-start | bytes 262144 | tf_op jit(solution)/shard_map/all_to_all | solution.py:321

commit v2 on v1

--- a/solution.py
+++ b/solution.py
@@ -9,6 +9,7 @@
 from jax.sharding import PartitionSpec as P
 
 HALO = 64
+MXU = True
 LANES = 128
 AXES = ("comp", "tile")
 
@@ -135,28 +136,25 @@
 
 
 def rim_kernel(first, last, head, tail):
-    nfreq = first.shape[0]
     half = head.shape[0]
-    for f in range(half):
+    for d in range(half):
         lane = lax.broadcasted_iota(jnp.int32, first.shape[1:], 1)
-        g = min(f + half, nfreq - 1)
-        head[f] = jnp.where(lane < HALO, first[f], pltpu.roll(first[g], HALO, 1))
-        tail[f] = jnp.where(lane >= HALO, last[f], pltpu.roll(last[g], HALO, 1))
+        head[d] = jnp.where(lane < HALO, first[d], pltpu.roll(first[d + half], HALO, 1))
+        tail[d] = jnp.where(lane >= HALO, last[d], pltpu.roll(last[d + half], HALO, 1))
 
 
 def wave_kernel(
-    spectrum, before, after, nbr, mask, wind_u, wind_v, spec_out, logz, tau, pad, new, sem_in, sem_out
+    spectrum, before, after, nbr, mask, wind_u, wind_v, spec_out, logz, tau, pad, new, parts, sem_in, sem_out
 ):
-    nfreq, ndir, width = spectrum.shape
+    ndir, nfreq, width = spectrum.shape
+    rows = parts.shape[1]
     blocks = width // LANES
     half = before.shape[0]
-    freq = (np.float32(0.0418) * np.float32(1.1) ** np.arange(nfreq, dtype=np.float32)).astype(np.float64)
-    courant = 0.7 * freq[0] / freq
-    sigma = freq / freq[-1]
+    quarter = ndir // 4
     theta = 2.0 * math.pi * (np.arange(ndir) + 0.5) / ndir
     cos, sin = np.cos(theta), np.sin(theta)
-    tiles = [(d, min(8, ndir - d)) for d in range(0, ndir, 8)]
     f32 = jnp.float32
+    spare = jnp.zeros((rows - nfreq, LANES), f32)
 
     def load(c):
         lanes = pl.ds(pl.multiple_of(c * LANES, LANES), LANES)
@@ -167,112 +165,124 @@
         lanes = pl.ds(pl.multiple_of(c * LANES, LANES), LANES)
         return pltpu.make_async_copy(new.at[:, :, lanes], spec_out.at[:, :, lanes], sem_out.at[c])
 
-    def column(values, d, n):
-        iota = lax.broadcasted_iota(jnp.int32, (n, LANES), 0)
-        result = jnp.full((n, LANES), float(values[d]), f32)
-        for i in range(1, n):
-            result = jnp.where(iota == i, float(values[d + i]), result)
-        return result
+    def split(c):
+        lanes = pl.ds(pl.multiple_of(c * LANES, LANES), LANES)
+        high = pl.ds(pl.multiple_of(2 * c * LANES, LANES), LANES)
+        low = pl.ds(pl.multiple_of(2 * c * LANES + LANES, LANES), LANES)
+        for d in range(ndir):
+            value = jnp.concatenate([pad[d, :, lanes], spare], axis=0)
+            first = value.astype(jnp.bfloat16)
+            parts[d, :, high] = first
+            parts[d, :, low] = (value - first.astype(f32)).astype(jnp.bfloat16)
 
     for c in range(blocks):
         load(c).start()
-    for f in range(half):
-        pad[f, :, 0:LANES] = before[f]
-        pad[f, :, width + LANES :] = after[f]
-        if f + half < nfreq:
-            pad[f + half, :, 0:LANES] = pltpu.roll(before[f], HALO, 1)
-            pad[f + half, :, width + LANES :] = pltpu.roll(after[f], HALO, 1)
+    for d in range(half):
+        pad[d, :, 0:LANES] = before[d]
+        pad[d, :, width + LANES :] = after[d]
+        pad[d + half, :, 0:LANES] = pltpu.roll(before[d], HALO, 1)
+        pad[d + half, :, width + LANES :] = pltpu.roll(after[d], HALO, 1)
+    if MXU:
+        split(0)
+        split(blocks + 1)
     load(0).wait()
+    if MXU:
+        split(1)
+
+    step = lax.broadcasted_iota(jnp.int32, (nfreq, LANES), 0).astype(f32)
+    scale = jnp.exp(step * math.log(1.1))
+    courant = 0.7 / scale
+    sigma = scale * float(1.1 ** (1 - nfreq))
+    rate = sigma * scale * 0.0418
 
     def advance(j, carry):
         @pl.when(j < blocks - 1)
         def _():
             load(j + 1).wait()
+            if MXU:
+                split(j + 2)
 
         at = pl.multiple_of(j * LANES, LANES)
         here = pl.ds(at, LANES)
-        west = nbr[0:1, here] - HALO - at
-        east = nbr[1:2, here] - HALO - at
-        south = nbr[2:3, here] - HALO - at
-        north = nbr[3:4, here] - HALO - at
+        middle = pl.ds(pl.multiple_of(at + LANES, LANES), LANES)
+        rels = [nbr[i : i + 1, here] - HALO - at for i in range(4)]
         wu = wind_u[pl.ds(j, 1), :]
         wv = wind_v[pl.ds(j, 1), :]
         fm = mask[pl.ds(j, 1), :].astype(f32)
 
-        def block(shift, f, d, n):
-            return pad[f, d : d + n, pl.ds(pl.multiple_of(at + shift * LANES, LANES), LANES)]
-
-        energy = jnp.zeros((1, LANES), f32)
-        push = jnp.zeros((1, LANES), f32)
-        drives = []
-        for d, n in tiles:
-            iota = lax.broadcasted_iota(jnp.int32, (n, LANES), 0) + d
-
-            def way(values, low, high):
-                lows = [bool(values[d + i] > 0) for i in range(n)]
-                if all(lows):
-                    rel, pick = jnp.broadcast_to(low, (n, LANES)), 0
-                elif not any(lows):
-                    rel, pick = jnp.broadcast_to(high, (n, LANES)), 2
-                else:
-                    edge = next(i for i in range(1, n) if lows[i] != lows[0])
-                    pick = (iota < d + edge) if lows[0] else (iota >= d + edge)
-                    rel = jnp.where(pick, low, high)
-                own = jnp.logical_and(rel >= 0, rel < LANES)
-                return own, jnp.bitwise_and(rel, LANES - 1), pick
-
-            own_x, at_x, pick_x = way(cos, west, east)
-            own_y, at_y, pick_y = way(sin, south, north)
-            wide = jnp.abs(column(cos, d, n))
-            tall = jnp.abs(column(sin, d, n))
-            drive = 0.63 * (wu * column(cos, d, n) + wv * column(sin, d, n))
-            drives.append(drive)
-            total = jnp.zeros((n, LANES), f32)
-            total_push = jnp.zeros((n, LANES), f32)
-            for f in range(nfreq):
-                cell = block(1, f, d, n)
-
-                def upwind(own, index, pick):
-                    if isinstance(pick, int):
-                        other = block(pick, f, d, n)
-                    else:
-                        other = jnp.where(pick, block(0, f, d, n), block(2, f, d, n))
+        def pick(rel, block):
+            iota = lax.broadcasted_iota(jnp.int32, (LANES, LANES), 0) + block * LANES
+            hot = jnp.where(iota == rel, 1.0, 0.0).astype(jnp.bfloat16)
+            return jnp.concatenate([hot, hot], axis=0)
+
+        if MXU:
+            zero = jnp.zeros((2 * LANES, LANES), jnp.bfloat16)
+            low_x, low_y = [pick(rels[0], b) for b in (-1, 0)], [pick(rels[2], b) for b in (-1, 0)]
+            high_x, high_y = [pick(rels[1], b) for b in (0, 1)], [pick(rels[3], b) for b in (0, 1)]
+            tables = [
+                (0, list(zip(low_x, low_y))),
+                (0, list(zip([zero] + high_x, low_y + [zero]))),
+                (1, list(zip(high_x, high_y))),
+                (0, list(zip(low_x + [zero], [zero] + high_y))),
+            ]
+            picked = []
+            for q, (skip, table) in enumerate(tables):
+                table = jnp.concatenate([jnp.concatenate(pair, axis=1) for pair in table], axis=0)
+                lanes = pl.ds(pl.multiple_of(2 * at + 2 * LANES * skip, LANES), table.shape[0])
+                window = parts[q * quarter : (q + 1) * quarter, :, lanes]
+                window = window.reshape(quarter * rows, table.shape[0])
+                both = jnp.dot(window, table, preferred_element_type=f32)
+                picked.append(both.reshape(quarter, rows, 2 * LANES))
+        else:
+            full = [jnp.broadcast_to(rel, (nfreq, LANES)) for rel in rels]
+            owns = [jnp.logical_and(rel >= 0, rel < LANES) for rel in full]
+            index = [jnp.bitwise_and(rel, LANES - 1) for rel in full]
+            left = pl.ds(at, LANES)
+            right = pl.ds(pl.multiple_of(at + 2 * LANES, LANES), LANES)
+
+        total = jnp.zeros((nfreq, LANES), f32)
+        push = jnp.zeros((nfreq, LANES), f32)
+        for d in range(ndir):
+            cell = pad[d, :, middle]
+            if MXU:
+                both = picked[d // quarter][d % quarter, 0:nfreq, :]
+                upx, upy = both[:, :LANES], both[:, LANES:]
+            else:
+
+                def upwind(way):
+                    other = pad[d, :, right if way % 2 else left]
                     return jnp.where(
-                        own,
-                        jnp.take_along_axis(cell, index, axis=1, mode="promise_in_bounds"),
-                        jnp.take_along_axis(other, index, axis=1, mode="promise_in_bounds"),
+                        owns[way],
+                        jnp.take_along_axis(cell, index[way], axis=1, mode="promise_in_bounds"),
+                        jnp.take_along_axis(other, index[way], axis=1, mode="promise_in_bounds"),
                     )
 
-                upx = upwind(own_x, at_x, pick_x)
-                upy = upwind(own_y, at_y, pick_y)
-                moved = cell + float(courant[f]) * (wide * (upx - cell) + tall * (upy - cell))
-                new[f, d : d + n, here] = moved
-                total = total + moved
-                gain = jnp.maximum(0.0, float(sigma[f] * freq[f]) * drive - float(sigma[f]))
-                total_push = total_push + gain * moved
-            energy = energy + jnp.sum(total, axis=0, keepdims=True)
-            push = push + jnp.sum(total_push, axis=0, keepdims=True)
-
-        energy = energy / float(nfreq * ndir)
-        damp = fm * (0.5 * energy / (1.0 + energy))
+                upx = upwind(0 if cos[d] > 0 else 1)
+                upy = upwind(2 if sin[d] > 0 else 3)
+            change = float(abs(cos[d])) * (upx - cell) + float(abs(sin[d])) * (upy - cell)
+            moved = cell + courant * change
+            new[d, :, here] = moved
+            total = total + moved
+            drive = 0.63 * (wu * float(cos[d]) + wv * float(sin[d]))
+            push = push + jnp.maximum(0.0, rate * drive - sigma) * moved
+
+        energy = jnp.sum(total, axis=0, keepdims=True) / float(nfreq * ndir)
+        push = jnp.sum(push, axis=0, keepdims=True) / float(nfreq * ndir)
         speed = jnp.maximum(jnp.sqrt(wu * wu + wv * wv), 1.0)
         ustar0 = 0.035 * speed
-        tau_wave = fm * (push / float(nfreq * ndir))
+        tau_wave = fm * push
         ratio = jnp.minimum(tau_wave / (ustar0 * ustar0), 0.9)
         z0 = 0.01 / jnp.sqrt(1.0 - ratio) * ustar0 * ustar0 / 9.81 + 1.5e-05
         ustar = 0.4 * speed / jnp.log(10.0 / z0)
         logz[pl.ds(j, 1), :] = jnp.log(z0)
         tau[pl.ds(j, 1), :] = ustar * ustar
-        for (d, n), drive in zip(tiles, drives):
-            drive = drive * fm
-            fmb = jnp.broadcast_to(fm, (n, LANES))
-            dampb = jnp.broadcast_to(damp, (n, LANES))
-            for f in range(nfreq):
-                gain = jnp.maximum(
-                    0.0, float(0.3 * sigma[f] * freq[f]) * drive - float(0.3 * sigma[f]) * fmb
-                )
-                growth = fmb - float(sigma[f]) * dampb + gain
-                new[f, d : d + n, here] = new[f, d : d + n, here] * growth
+        base = fm - sigma * (fm * (0.5 * energy / (1.0 + energy)))
+        floor = (0.3 * sigma) * fm
+        steep = 0.3 * rate
+        for d in range(ndir):
+            drive = fm * (0.63 * (wu * float(cos[d]) + wv * float(sin[d])))
+            growth = base + jnp.maximum(0.0, steep * drive - floor)
+            new[d, :, here] = new[d, :, here] * growth
         store(j).start()
         return carry
 
@@ -290,18 +300,19 @@
     atm_u, atm_v, mixing, drag_prev, spectrum, sea_mask, wave_source, column_target, neighbours
 ):
     lev, columns = atm_u.shape
-    nfreq, ndir, width = spectrum.shape
+    spectrum = spectrum.transpose(1, 0, 2)
+    ndir, nfreq, width = spectrum.shape
     devices = lax.axis_size("comp") * lax.axis_size("tile")
     blocks = columns // LANES
-    half = (nfreq + 1) // 2
+    half, rows = ndir // 2, -(-nfreq // 16) * 16
     f32 = jnp.float32
     params = pltpu.CompilerParams(vmem_limit_bytes=LIMIT)
     square = jax.ShapeDtypeStruct((blocks, LANES), f32)
     box = jax.ShapeDtypeStruct((devices, 8, LANES), f32)
 
-    rim = jax.ShapeDtypeStruct((half, ndir, LANES), f32)
-    edge = lambda at: pl.BlockSpec((nfreq, ndir, LANES), lambda i: (0, 0, at))
-    whole = pl.BlockSpec((half, ndir, LANES), lambda i: (0, 0, 0))
+    rim = jax.ShapeDtypeStruct((half, nfreq, LANES), f32)
+    edge = lambda at: pl.BlockSpec((ndir, nfreq, LANES), lambda i: (0, 0, at))
+    whole = pl.BlockSpec((half, nfreq, LANES), lambda i: (0, 0, 0))
     head, tail = pl.pallas_call(
         rim_kernel,
         grid=(1,),
@@ -341,8 +352,9 @@
         out_specs=[ANY, VMEM, VMEM],
         out_shape=[jax.ShapeDtypeStruct(spectrum.shape, f32), square, square],
         scratch_shapes=[
-            pltpu.VMEM((nfreq, ndir, width + 2 * LANES), f32),
-            pltpu.VMEM((nfreq, ndir, width), f32),
+            pltpu.VMEM((ndir, nfreq, width + 2 * LANES), f32),
+            pltpu.VMEM((ndir, nfreq, width), f32),
+            pltpu.VMEM((ndir, rows, 2 * width + 4 * LANES), jnp.bfloat16),
             pltpu.SemaphoreType.DMA((blocks,)),
             pltpu.SemaphoreType.DMA((blocks,)),
         ],
@@ -352,6 +364,7 @@
         ),
     )(spectrum, before, after, neighbours, sea_mask.reshape(blocks, LANES), wind_u, wind_v)
     rough, stress = relay(wave_source, logz, tau)
+    spectrum_new = spectrum_new.transpose(1, 0, 2)
     return (u_new, v_new, spectrum_new, rough.reshape(columns), stress.reshape(columns))
 
 

time: 84.5 us -> 54.8 us (0.65)
  local copies, waits for them, and re-layouts: 24.8 us -> 0.06 us
  Pallas kernels: 35 us -> 24.1 us
  waiting for transfers between devices: 0.01 us -> 6.67 us
    unnamed x18 -> x16, local copies, waits for them, and re-layouts: 24.8 us -> 0.04 us
    pallas_call x1, Pallas kernels: 28.7 us -> 17.7 us  [local(): pl.pallas_call(wave_kernel, in_specs=[ANY] + [VMEM] * 6, out_specs=[ANY,...]
    all_to_all x1, waiting for transfers between devices: 0.01 us -> 6.66 us  [relay(): lax.all_to_all(outbox, AXES, split_axis=0, concat_axis=0, tiled=True)]
  transfers between devices with their start and end apart: 3 -> 3, of which waited for: 0 -> 1; matrix products, arithmetic and copies ran while one was open for 15% -> 0% of each run, Pallas kernels for 3% -> 4%
where the time goes in v2:
time: 54.8 us; the launch traced here: 54.6 us
  Pallas kernels  24.1 us (44%)
  blocking collectives  12.7 us (23%)
  starting transfers between devices  10.2 us (19%)
  waiting for transfers between devices  6.67 us (12%)
  between operations  0.82 us (1%)
    pallas_call x1, Pallas kernels, local(): pl.pallas_call(wave_kernel, in_specs=[ANY] + [VMEM] * 6, out_specs=[ANY,...  17.7 us
    all_to_all x1, blocking collectives, relay(): lax.all_to_all(outbox, AXES, split_axis=0, concat_axis=0, tiled=True)  12.7 us
    all_to_all x1, waiting for transfers between devices, relay(): lax.all_to_all(outbox, AXES, split_axis=0, concat_axis=0, tiled=True)  6.66 us
    all_to_all x1, starting transfers between devices, relay(): lax.all_to_all(outbox, AXES, split_axis=0, concat_axis=0, tiled=True)  3.74 us
    ppermute x1, starting transfers between devices, local(): after = lax.ppermute(head, AXES, [(b, a) for a, b in up])  3.5 us
    ppermute x1, starting transfers between devices, local(): before = lax.ppermute(tail, AXES, up)  3 us
    pallas_call x2, Pallas kernels, relay(): pl.pallas_call(pack_kernel, in_specs=[VMEM] * 3, out_specs=VMEM, out_shap...  2.28 us
    pallas_call x1, Pallas kernels, local(): pl.pallas_call(rim_kernel, grid=(1,), in_specs=[edge(0), edge(width // LA...  1.54 us
  transfers between devices with their start and end apart: 3, of which 1 were waited for; matrix products, arithmetic and copies ran while one was open for 0% of the time, Pallas kernels for 4%

profile of v2, /device:TPU:0, one launch (start us, length us, event | category | flops | bytes accessed | tf_op | source)
XLA Modules:
  0.0 54.6 jit_solution(4634651308548602793)
XLA Ops:
  0.6 0.0 copy-start
  0.6 0.0 copy-start.1
  0.7 0.0 copy-start.5
  0.7 0.0 copy-start.3
  0.7 0.0 copy-start.7
  0.7 1.5 %shard_map.129 = (f32[18,29,128]{2,1,0:T(8,128)S(1)}, f32[18,29,128]{2,1,0:T(8,128)S(1)}) custom-call(f32[36,29,2048]{2,1,0:T(8,128)} %bitcast.16, f32[36,29,2048]{2,1,0:T(8,128)} %bitcast.17), custom_call_target="tpu_custom_call" | custom-call | tf_op jit(solution)/shard_map/pallas_call | solution.py:316
  2.2 0.0 copy-start.6
  2.2 0.0 copy-start.2
  2.3 0.0 copy-start.4
  2.3 3.0 %collective-permute-start = (f32[18,29,128]{2,1,0:T(8,128)S(1)}, f32[18,29,128]{2,1,0:T(8,128)S(1)}, u32[]{:S(2)}, u32[]{:S(2)}) collective-permute-start(f32[18,29,128]{2,1,0:T(8,128)S(1)} %get-tuple-element.18), channel_id=1, source_target_pairs={{0,1},{1,2},{2,3},{3,4},{4,5},{5,6},{6,7},{7,8},{8,9},{9,10},{10,1... | collective-permute-start | bytes 801800 | tf_op jit(solution)/shard_map/ppermute | solution.py:325
  5.3 3.5 %collective-permute-start.1 = (f32[18,29,128]{2,1,0:T(8,128)S(1)}, f32[18,29,128]{2,1,0:T(8,128)S(1)}, u32[]{:S(2)}, u32[]{:S(2)}) collective-permute-start(f32[18,29,128]{2,1,0:T(8,128)S(1)} %get-tuple-element.19), channel_id=1, source_target_pairs={{1,0},{2,1},{3,2},{4,3},{5,4},{6,5},{7,6},{8,7},{9,8},{10,9},{11,1... | collective-permute-start | bytes 801800 | tf_op jit(solution)/shard_map/ppermute | solution.py:326
  8.8 0.0 copy-done
  8.8 0.0 copy-done.1
  8.8 0.0 copy-done.5
  8.8 0.8 %shard_map.130 = f32[32,8,128]{2,1,0:T(8,128)S(1)} custom-call(s32[16,128]{1,0:T(8,128)S(1)} %bitcast.13, f32[16,128]{1,0:T(8,128)S(1)} %bitcast.10, f32[16,128]{1,0:T(8,128)S(1)} %bitcast.11), custom_call_target="tpu_custom_call" | custom-call | tf_op jit(solution)/shard_map/pallas_call | solution.py:329
  9.6 12.7 %all_to_all.10.inbox = f32[32,8,128]{2,1,0:T(8,128)S(1)} all-to-all(f32[32,8,128]{2,1,0:T(8,128)S(1)} %shard_map.130), channel_id=1, replica_groups=mesh['comp'=4,'tile'=8] {'comp','tile'}, dimensions={0} | all-to-all | bytes 262144 | tf_op jit(solution)/shard_map/all_to_all | solution.py:332
  22.3 0.4 shard_map.131
  22.8 0.0 collective-permute-done.before
  22.8 0.0 collective-permute-done.1.after
  22.8 0.0 copy-done.3
  22.8 0.0 copy-done.7
  22.8 17.7 %shard_map.132 = (f32[36,29,2048]{2,1,0:T(8,128)}, f32[16,128]{1,0:T(8,128)S(1)}, f32[16,128]{1,0:T(8,128)S(1)}) custom-call(f32[36,29,2048]{2,1,0:T(8,128)} %bitcast.18, f32[18,29,128]{2,1,0:T(8,128)S(1)} %collective-permute-done.before, f32[18,29,128]{2,1,0:T(8,128)S(1)} %collective-permute-done.1.after, s32[4,2048]{1,0:T(4,128)S(1)} %copy-done.3, ...), custom_call_target="tpu_custom_call" | custom-call | flops 64143360 | bytes 17104896 | tf_op jit(solution)/shard_map/pallas_call | solution.py:349
  40.5 0.0 copy-done.6
  40.6 1.5 %shard_map.133 = f32[32,8,128]{2,1,0:T(8,128)} custom-call(s32[16,128]{1,0:T(8,128)S(1)} %bitcast.14, f32[16,128]{1,0:T(8,128)S(1)} %get-tuple-element.23.first, f32[16,128]{1,0:T(8,128)S(1)} %get-tuple-element.24.second), custom_call_target="tpu_custom_call" | custom-call | tf_op jit(solution)/shard_map/pallas_call | solution.py:329
  42.0 3.7 %all-to-all-start.1 = ((f32[32,8,128]{2,1,0:T(8,128)}), f32[32,8,128]{2,1,0:T(8,128)S(1)}, u32[]{:S(2)}, u32[]{:S(2)}) async-start(f32[32,8,128]{2,1,0:T(8,128)} %shard_map.133), calls=%async_computation.1 | async-start | bytes 262144 | tf_op jit(solution)/shard_map/all_to_all | solution.py:332
  45.8 0.0 copy-done.2
  45.8 0.0 copy-done.4
  45.8 1.1 %shard_map.128 = (f32[20,2048]{1,0:T(8,128)}, f32[20,2048]{1,0:T(8,128)}) custom-call(f32[20,2048]{1,0:T(8,128)S(1)} %copy-done, f32[20,2048]{1,0:T(8,128)S(1)} %copy-done.1, f32[19,2048]{1,0:T(8,128)S(1)} %copy-done.2, f32[1,2048]{1,0:T(1,128)S(1)} %bitcast.12), custom_call_target="tpu_custom_call" | custom-call | flops 819200 | bytes 819200 | tf_op jit(solution)/shard_map/pallas_call | solution.py:341
  46.8 6.7 %all-to-all-done.1.inbox = f32[32,8,128]{2,1,0:T(8,128)S(1)} async-done(((f32[32,8,128]{2,1,0:T(8,128)}), f32[32,8,128]{2,1,0:T(8,128)S(1)}, u32[]{:S(2)}, u32[]{:S(2)}) %all-to-all-start.1) | async-done | bytes 131104 | tf_op jit(solution)/shard_map/all_to_all | solution.py:332
  53.5 1.0 %shard_map.134 = (f32[16,128]{1,0:T(8,128)}, f32[16,128]{1,0:T(8,128)}) custom-call(f32[32,8,128]{2,1,0:T(8,128)S(1)} %all-to-all-done.1.inbox), custom_call_target="tpu_custom_call" | custom-call | tf_op jit(solution)/shard_map/pallas_call | solution.py:333
  (2 shorter events, 0.0 us)
Async XLA Ops:
  0.6 8.1 %copy-start = (f32[20,2048]{1,0:T(8,128)S(1)}, f32[20,2048]{1,0:T(8,128)}, u32[]{:S(2)}) copy-start(f32[20,2048]{1,0:T(8,128)} %u_ref.1) | copy-start | bytes 491524
  0.6 8.1 %copy-start.1 = (f32[20,2048]{1,0:T(8,128)S(1)}, f32[20,2048]{1,0:T(8,128)}, u32[]{:S(2)}) copy-start(f32[20,2048]{1,0:T(8,128)} %v_ref.1) | copy-start | bytes 491524
  0.7 8.2 %copy-start.5 = (s32[2048]{0:T(1024)S(1)}, s32[2048]{0:T(1024)}, u32[]{:S(2)}) copy-start(s32[2048]{0:T(1024)} %param.16) | copy-start | bytes 24580
  0.7 22.1 %copy-start.3 = (s32[4,2048]{1,0:T(4,128)S(1)}, s32[4,2048]{1,0:T(4,128)}, u32[]{:S(2)}) copy-start(s32[4,2048]{1,0:T(4,128)} %nbr.1) | copy-start | bytes 98308
  0.7 22.1 %copy-start.7 = (s32[2048]{0:T(1024)S(1)}, s32[2048]{0:T(1024)}, u32[]{:S(2)}) copy-start(s32[2048]{0:T(1024)} %param.14) | copy-start | bytes 24580
  2.2 38.3 %copy-start.6 = (s32[2048]{0:T(1024)S(1)}, s32[2048]{0:T(1024)}, u32[]{:S(2)}) copy-start(s32[2048]{0:T(1024)} %param.15) | copy-start | bytes 24580
  2.2 43.5 %copy-start.2 = (f32[19,2048]{1,0:T(8,128)S(1)}, f32[19,2048]{1,0:T(8,128)}, u32[]{:S(2)}) copy-start(f32[19,2048]{1,0:T(8,128)} %mixing.1) | copy-start | bytes 466948
  2.3 43.5 %copy-start.4 = (f32[2048]{0:T(1024)S(1)}, f32[2048]{0:T(1024)}, u32[]{:S(2)}) copy-start(f32[2048]{0:T(1024)} %param.12) | copy-start | bytes 24580
  2.3 20.5 %collective-permute-start = (f32[18,29,128]{2,1,0:T(8,128)S(1)}, f32[18,29,128]{2,1,0:T(8,128)S(1)}, u32[]{:S(2)}, u32[]{:S(2)}) collective-permute-start(f32[18,29,128]{2,1,0:T(8,128)S(1)} %get-tuple-element.18), channel_id=1, source_target_pairs={{0,1},{1,2},{2,3},{3,4},{4,5},{5,6},{6,7},{7,8},{8,9},{9,10},{10,1... | collective-permute-start | bytes 801800 | tf_op jit(solution)/shard_map/ppermute | solution.py:325
  5.3 17.5 %collective-permute-start.1 = (f32[18,29,128]{2,1,0:T(8,128)S(1)}, f32[18,29,128]{2,1,0:T(8,128)S(1)}, u32[]{:S(2)}, u32[]{:S(2)}) collective-permute-start(f32[18,29,128]{2,1,0:T(8,128)S(1)} %get-tuple-element.19), channel_id=1, source_target_pairs={{1,0},{2,1},{3,2},{4,3},{5,4},{6,5},{7,6},{8,7},{9,8},{10,9},{11,1... | collective-permute-start | bytes 801800 | tf_op jit(solution)/shard_map/ppermute | solution.py:326
  42.0 11.5 %all-to-all-start.1 = ((f32[32,8,128]{2,1,0:T(8,128)}), f32[32,8,128]{2,1,0:T(8,128)S(1)}, u32[]{:S(2)}, u32[]{:S(2)}) async-start(f32[32,8,128]{2,1,0:T(8,128)} %shard_map.133), calls=%async_computation.1 | async-start | bytes 262144 | tf_op jit(solution)/shard_map/all_to_all | solution.py:332

commit v3 on v2

--- a/solution.py
+++ b/solution.py
@@ -1,3 +1,4 @@
+import functools
 import math
 
 import jax
@@ -101,6 +102,61 @@
     first[...], second[...] = empty_inbox(inbox, first.shape[0])
 
 
+def exchange_kernel(count, tiles, *refs):
+    rims = len(refs) > 4
+    if rims:
+        outbox, head, tail, inbox, before, after, sent, got, rim_sent, rim_got = refs
+    else:
+        outbox, inbox, sent, got = refs
+    me = lax.axis_index("comp") * tiles + lax.axis_index("tile")
+
+    def name(index):
+        return (index // tiles, index % tiles)
+
+    def move(source, target, send, receive, device):
+        return pltpu.make_async_remote_copy(
+            src_ref=source,
+            dst_ref=target,
+            send_sem=send,
+            recv_sem=receive,
+            device_id=name(device),
+            device_id_type=pl.DeviceIdType.MESH,
+        )
+
+    barrier = pltpu.get_barrier_semaphore()
+
+    def greet(step, carry):
+        pl.semaphore_signal(
+            barrier, inc=1, device_id=name((me + step) % count), device_id_type=pl.DeviceIdType.MESH
+        )
+        return carry
+
+    lax.fori_loop(1, count, greet, 0)
+    pl.semaphore_wait(barrier, count - 1)
+
+    def start(step, carry):
+        peer = (me + step) % count
+        move(outbox.at[peer], inbox.at[me], sent.at[peer], got.at[me], peer).start()
+        return carry
+
+    def finish(step, carry):
+        peer = (me + step) % count
+        move(outbox.at[peer], inbox.at[peer], sent.at[peer], got.at[peer], peer).wait()
+        return carry
+
+    lax.fori_loop(1, count, start, 0)
+    if rims:
+        up = move(tail, before, rim_sent.at[0], rim_got.at[0], (me + 1) % count)
+        down = move(head, after, rim_sent.at[1], rim_got.at[1], (me + count - 1) % count)
+        up.start()
+        down.start()
+    inbox[me] = outbox[me]
+    lax.fori_loop(1, count, finish, 0)
+    if rims:
+        up.wait()
+        down.wait()
+
+
 def solve_kernel(u_ref, v_ref, mixing, drag, u_out, v_out):
     lev = u_ref.shape[0]
     cps = []
@@ -308,7 +364,7 @@
     f32 = jnp.float32
     params = pltpu.CompilerParams(vmem_limit_bytes=LIMIT)
     square = jax.ShapeDtypeStruct((blocks, LANES), f32)
-    box = jax.ShapeDtypeStruct((devices, 8, LANES), f32)
+    box = jax.ShapeDtypeStruct((devices, 4, LANES), f32)
 
     rim = jax.ShapeDtypeStruct((half, nfreq, LANES), f32)
     edge = lambda at: pl.BlockSpec((ndir, nfreq, LANES), lambda i: (0, 0, at))
@@ -321,22 +377,37 @@
         out_shape=[rim, rim],
         compiler_params=params,
     )(spectrum, spectrum)
-    up = [(i, (i + 1) % devices) for i in range(devices)]
-    before = lax.ppermute(tail, AXES, up)
-    after = lax.ppermute(head, AXES, [(b, a) for a, b in up])
-
-    def relay(target, first, second):
-        outbox = pl.pallas_call(
-            pack_kernel, in_specs=[VMEM] * 3, out_specs=VMEM, out_shape=box, compiler_params=params
+    plain = dict(compiler_params=params)
+
+    def exchange(index, box_out, *sides):
+        shapes = [box] + [rim] * len(sides)
+        sems = [pltpu.SemaphoreType.DMA((devices,))] * 2
+        if sides:
+            sems = sems + [pltpu.SemaphoreType.DMA((2,))] * 2
+        return pl.pallas_call(
+            functools.partial(exchange_kernel, devices, lax.axis_size("tile")),
+            in_specs=[VMEM] * len(shapes),
+            out_specs=[VMEM] * len(shapes),
+            out_shape=shapes,
+            scratch_shapes=sems,
+            compiler_params=pltpu.CompilerParams(
+                collective_id=index, has_side_effects=True, vmem_limit_bytes=LIMIT
+            ),
+        )(box_out, *sides)
+
+    def pack(target, first, second):
+        return pl.pallas_call(
+            pack_kernel, in_specs=[VMEM] * 3, out_specs=VMEM, out_shape=box, **plain
         )(target.reshape(blocks, LANES), first, second)
-        inbox = lax.all_to_all(outbox, AXES, split_axis=0, concat_axis=0, tiled=True)
+
+    def unpack(inbox):
         return pl.pallas_call(
-            unpack_kernel, in_specs=[VMEM], out_specs=[VMEM] * 2, out_shape=[square] * 2, compiler_params=params
+            unpack_kernel, in_specs=[VMEM], out_specs=[VMEM] * 2, out_shape=[square] * 2, **plain
         )(inbox)
 
-    wind_u, wind_v = relay(
-        column_target, atm_u[-1].reshape(blocks, LANES), atm_v[-1].reshape(blocks, LANES)
-    )
+    outbox = pack(column_target, atm_u[-1].reshape(blocks, LANES), atm_v[-1].reshape(blocks, LANES))
+    inbox, before, after = exchange(0, outbox, head, tail)
+    wind_u, wind_v = unpack(inbox)
     slab = jax.ShapeDtypeStruct((lev, columns), f32)
     u_new, v_new = pl.pallas_call(
         solve_kernel,
@@ -363,7 +434,7 @@
             flops=30 * spectrum.size, bytes_accessed=8 * spectrum.size, transcendentals=0
         ),
     )(spectrum, before, after, neighbours, sea_mask.reshape(blocks, LANES), wind_u, wind_v)
-    rough, stress = relay(wave_source, logz, tau)
+    rough, stress = unpack(exchange(1, pack(wave_source, logz, tau))[0])
     spectrum_new = spectrum_new.transpose(1, 0, 2)
     return (u_new, v_new, spectrum_new, rough.reshape(columns), stress.reshape(columns))
 

time: 54.8 us -> 54.8 us (level)
  Pallas kernels: 24.1 us -> 53.7 us
  blocking collectives: 12.7 us -> 0 us
  starting transfers between devices: 10.2 us -> 0 us
  waiting for transfers between devices: 6.67 us -> 0 us
    pallas_call x4 -> x6, Pallas kernels: 3.75 us -> 33.4 us  [the longest x2 30.3 us: exchange(): pl.pallas_call(functools.partial(exchange_kernel, devices, lax.axis_size(...]
    all_to_all x1 -> x0, blocking collectives: 12.7 us -> none  [relay(): lax.all_to_all(outbox, AXES, split_axis=0, concat_axis=0, tiled=True)]
    all_to_all x1 -> x0, waiting for transfers between devices: 6.66 us -> none  [relay(): lax.all_to_all(outbox, AXES, split_axis=0, concat_axis=0, tiled=True)]
    ppermute x2 -> x0, starting transfers between devices: 6.5 us -> none  [the longest x1 3.5 us: local(): after = lax.ppermute(head, AXES, [(b, a) for a, b in up])]
    all_to_all x1 -> x0, starting transfers between devices: 3.74 us -> none  [relay(): lax.all_to_all(outbox, AXES, split_axis=0, concat_axis=0, tiled=True)]
  transfers between devices with their start and end apart: 3 -> 0, of which waited for: 1 -> 0; matrix products, arithmetic and copies ran while one was open for 0% -> 0% of each run, Pallas kernels for 4% -> 0%
where the time goes in v3:
time: 54.8 us; the launch traced here: 54.6 us
  Pallas kernels  53.7 us (98%)
  between operations  0.8 us (1%)
    pallas_call x2, Pallas kernels, exchange(): pl.pallas_call(functools.partial(exchange_kernel, devices, lax.axis_size(...  30.3 us
    pallas_call x1, Pallas kernels, local(): pl.pallas_call(wave_kernel, in_specs=[ANY] + [VMEM] * 6, out_specs=[ANY,...  17.7 us
    pallas_call x2, Pallas kernels, pack(): pl.pallas_call(pack_kernel, in_specs=[VMEM] * 3, out_specs=VMEM, out_shap...  1.62 us
    pallas_call x1, Pallas kernels, local(): pl.pallas_call(rim_kernel, grid=(1,), in_specs=[edge(0), edge(width // LA...  1.54 us
    pallas_call x2, Pallas kernels, unpack(): pl.pallas_call(unpack_kernel, in_specs=[VMEM], out_specs=[VMEM] * 2, out_...  1.47 us

profile of v3, /device:TPU:0, one launch (start us, length us, event | category | flops | bytes accessed | tf_op | source)
XLA Modules:
  0.0 54.6 jit_solution(14339477533548271945)
XLA Ops:
  0.6 0.0 copy-start
  0.6 0.0 copy-start.1
  0.7 0.0 copy-start.5
  0.7 0.0 copy-start.3
  0.7 0.0 copy-start.7
  0.7 1.5 %shard_map.130 = (f32[18,29,128]{2,1,0:T(8,128)S(1)}, f32[18,29,128]{2,1,0:T(8,128)S(1)}) custom-call(f32[36,29,2048]{2,1,0:T(8,128)} %bitcast.16, f32[36,29,2048]{2,1,0:T(8,128)} %bitcast.17), custom_call_target="tpu_custom_call" | custom-call | tf_op jit(solution)/shard_map/pallas_call | solution.py:372
  2.2 0.0 copy-start.6
  2.2 0.0 copy-start.2
  2.3 0.0 copy-start.4
  2.3 0.0 copy-done
  2.3 0.0 copy-done.1
  2.3 0.0 copy-done.5
  2.3 0.8 %shard_map.129.refs_0_ = f32[32,4,128]{2,1,0:T(4,128)S(1)} custom-call(s32[16,128]{1,0:T(8,128)S(1)} %bitcast.13, f32[16,128]{1,0:T(8,128)S(1)} %bitcast.10, f32[16,128]{1,0:T(8,128)S(1)} %bitcast.11), custom_call_target="tpu_custom_call" | custom-call | tf_op jit(solution)/shard_map/pallas_call | solution.py:399
  3.2 21.7 %shard_map.131 = (f32[32,4,128]{2,1,0:T(4,128)S(1)}, f32[18,29,128]{2,1,0:T(8,128)S(1)}, f32[18,29,128]{2,1,0:T(8,128)S(1)}) custom-call(f32[32,4,128]{2,1,0:T(4,128)S(1)} %shard_map.129.refs_0_, f32[18,29,128]{2,1,0:T(8,128)S(1)} %get-tuple-element.21.refs_1_, f32[18,29,128]{2,1,0:T(8,128)S(1)} %get-tuple-element.22.refs_2_), custom_call_target="tpu_custom_call" | custom-call | tf_op jit(solution)/shard_map/pallas_call | solution.py:387
  24.9 0.4 shard_map.132
  25.3 0.0 copy-done.3
  25.3 0.0 copy-done.7
  25.3 17.7 %shard_map.133 = (f32[36,29,2048]{2,1,0:T(8,128)}, f32[16,128]{1,0:T(8,128)S(1)}, f32[16,128]{1,0:T(8,128)S(1)}) custom-call(f32[36,29,2048]{2,1,0:T(8,128)} %bitcast.18, f32[18,29,128]{2,1,0:T(8,128)S(1)} %get-tuple-element.23.before, f32[18,29,128]{2,1,0:T(8,128)S(1)} %get-tuple-element.24.after, s32[4,2048]{1,0:T(4,128)S(1)} %copy-done.3, ...), custom_call_target="tpu_custom_call" | custom-call | flops 64143360 | bytes 17104896 | tf_op jit(solution)/shard_map/pallas_call | solution.py:420
  43.1 0.0 copy-done.6
  43.1 0.8 %shard_map.134.refs_0_ = f32[32,4,128]{2,1,0:T(4,128)S(1)} custom-call(s32[16,128]{1,0:T(8,128)S(1)} %bitcast.14, f32[16,128]{1,0:T(8,128)S(1)} %get-tuple-element.29.first, f32[16,128]{1,0:T(8,128)S(1)} %get-tuple-element.30.second), custom_call_target="tpu_custom_call" | custom-call | tf_op jit(solution)/shard_map/pallas_call | solution.py:399
  43.9 8.6 %shard_map.135.inbox = f32[32,4,128]{2,1,0:T(4,128)S(1)} custom-call(f32[32,4,128]{2,1,0:T(4,128)S(1)} %shard_map.134.refs_0_), custom_call_target="tpu_custom_call" | custom-call | tf_op jit(solution)/shard_map/pallas_call | solution.py:387
  52.5 1.0 %shard_map.136 = (f32[16,128]{1,0:T(8,128)}, f32[16,128]{1,0:T(8,128)}) custom-call(f32[32,4,128]{2,1,0:T(4,128)S(1)} %shard_map.135.inbox), custom_call_target="tpu_custom_call" | custom-call | tf_op jit(solution)/shard_map/pallas_call | solution.py:404
  53.5 0.0 copy-done.2
  53.5 0.0 copy-done.4
  53.6 1.1 %shard_map.128 = (f32[20,2048]{1,0:T(8,128)}, f32[20,2048]{1,0:T(8,128)}) custom-call(f32[20,2048]{1,0:T(8,128)S(1)} %copy-done, f32[20,2048]{1,0:T(8,128)S(1)} %copy-done.1, f32[19,2048]{1,0:T(8,128)S(1)} %copy-done.2, f32[1,2048]{1,0:T(1,128)S(1)} %bitcast.12), custom_call_target="tpu_custom_call" | custom-call | flops 819200 | bytes 819200 | tf_op jit(solution)/shard_map/pallas_call | solution.py:412
  (2 shorter events, 0.0 us)
Async XLA Ops:
  0.6 1.6 %copy-start = (f32[20,2048]{1,0:T(8,128)S(1)}, f32[20,2048]{1,0:T(8,128)}, u32[]{:S(2)}) copy-start(f32[20,2048]{1,0:T(8,128)} %u_ref.1) | copy-start | bytes 491524
  0.6 1.7 %copy-start.1 = (f32[20,2048]{1,0:T(8,128)S(1)}, f32[20,2048]{1,0:T(8,128)}, u32[]{:S(2)}) copy-start(f32[20,2048]{1,0:T(8,128)} %v_ref.1) | copy-start | bytes 491524
  0.7 1.7 %copy-start.5 = (s32[2048]{0:T(1024)S(1)}, s32[2048]{0:T(1024)}, u32[]{:S(2)}) copy-start(s32[2048]{0:T(1024)} %param.16) | copy-start | bytes 24580
  0.7 24.7 %copy-start.3 = (s32[4,2048]{1,0:T(4,128)S(1)}, s32[4,2048]{1,0:T(4,128)}, u32[]{:S(2)}) copy-start(s32[4,2048]{1,0:T(4,128)} %nbr.1) | copy-start | bytes 98308
  0.7 24.7 %copy-start.7 = (s32[2048]{0:T(1024)S(1)}, s32[2048]{0:T(1024)}, u32[]{:S(2)}) copy-start(s32[2048]{0:T(1024)} %param.14) | copy-start | bytes 24580
  2.2 40.9 %copy-start.6 = (s32[2048]{0:T(1024)S(1)}, s32[2048]{0:T(1024)}, u32[]{:S(2)}) copy-start(s32[2048]{0:T(1024)} %param.15) | copy-start | bytes 24580
  2.2 51.3 %copy-start.2 = (f32[19,2048]{1,0:T(8,128)S(1)}, f32[19,2048]{1,0:T(8,128)}, u32[]{:S(2)}) copy-start(f32[19,2048]{1,0:T(8,128)} %mixing.1) | copy-start | bytes 466948
  2.3 51.3 %copy-start.4 = (f32[2048]{0:T(1024)S(1)}, f32[2048]{0:T(1024)}, u32[]{:S(2)}) copy-start(f32[2048]{0:T(1024)} %param.12) | copy-start | bytes 24580

commit v4 on v3

--- a/solution.py
+++ b/solution.py
@@ -199,13 +199,14 @@
         tail[d] = jnp.where(lane >= HALO, last[d], pltpu.roll(last[d + half], HALO, 1))
 
 
-def wave_kernel(
-    spectrum, before, after, nbr, mask, wind_u, wind_v, spec_out, logz, tau, pad, new, parts, sem_in, sem_out
-):
+def wave_kernel(edge, *refs):
+    if edge:
+        before, after, _, *refs = refs
+    spectrum, nbr, mask, wind_u, wind_v, spec_out, logz, tau, pad, new, parts, sem_in, sem_out = refs
     ndir, nfreq, width = spectrum.shape
     rows = parts.shape[1]
     blocks = width // LANES
-    half = before.shape[0]
+    half = ndir // 2
     quarter = ndir // 4
     theta = 2.0 * math.pi * (np.arange(ndir) + 0.5) / ndir
     cos, sin = np.cos(theta), np.sin(theta)
@@ -231,19 +232,21 @@
             parts[d, :, high] = first
             parts[d, :, low] = (value - first.astype(f32)).astype(jnp.bfloat16)
 
-    for c in range(blocks):
+    last = blocks - 1
+    near = (0, 1, last - 1, last) if edge else range(blocks)
+    for c in near:
         load(c).start()
-    for d in range(half):
-        pad[d, :, 0:LANES] = before[d]
-        pad[d, :, width + LANES :] = after[d]
-        pad[d + half, :, 0:LANES] = pltpu.roll(before[d], HALO, 1)
-        pad[d + half, :, width + LANES :] = pltpu.roll(after[d], HALO, 1)
-    if MXU:
+    if edge:
+        for d in range(half):
+            pad[d, :, 0:LANES] = before[d]
+            pad[d, :, width + LANES :] = after[d]
+            pad[d + half, :, 0:LANES] = pltpu.roll(before[d], HALO, 1)
+            pad[d + half, :, width + LANES :] = pltpu.roll(after[d], HALO, 1)
         split(0)
         split(blocks + 1)
-    load(0).wait()
-    if MXU:
-        split(1)
+    for c in near if edge else (0, 1):
+        load(c).wait()
+        split(c + 1)
 
     step = lax.broadcasted_iota(jnp.int32, (nfreq, LANES), 0).astype(f32)
     scale = jnp.exp(step * math.log(1.1))
@@ -252,11 +255,11 @@
     rate = sigma * scale * 0.0418
 
     def advance(j, carry):
-        @pl.when(j < blocks - 1)
-        def _():
+        if edge:
+            j = j * last
+        else:
             load(j + 1).wait()
-            if MXU:
-                split(j + 2)
+            split(j + 2)
 
         at = pl.multiple_of(j * LANES, LANES)
         here = pl.ds(at, LANES)
@@ -342,8 +345,9 @@
         store(j).start()
         return carry
 
-    lax.fori_loop(0, blocks, advance, 0)
-    for c in range(blocks):
+    first, stop = (0, 2) if edge else (1, last)
+    lax.fori_loop(first, stop, advance, 0)
+    for c in (0, last) if edge else range(1, last):
         store(c).wait()
 
 
@@ -406,7 +410,11 @@
         )(inbox)
 
     outbox = pack(column_target, atm_u[-1].reshape(blocks, LANES), atm_v[-1].reshape(blocks, LANES))
-    inbox, before, after = exchange(0, outbox, head, tail)
+    (inbox,) = exchange(0, outbox)
+    inbox, head, tail = lax.optimization_barrier((inbox, head, tail))
+    up = [(i, (i + 1) % devices) for i in range(devices)]
+    before = lax.ppermute(tail, AXES, up)
+    after = lax.ppermute(head, AXES, [(b, a) for a, b in up])
     wind_u, wind_v = unpack(inbox)
     slab = jax.ShapeDtypeStruct((lev, columns), f32)
     u_new, v_new = pl.pallas_call(
@@ -417,23 +425,36 @@
         compiler_params=params,
         cost_estimate=pl.CostEstimate(flops=20 * lev * columns, bytes_accessed=20 * lev * columns, transcendentals=0),
     )(atm_u, atm_v, mixing, drag_prev.reshape(1, columns))
-    spectrum_new, logz, tau = pl.pallas_call(
-        wave_kernel,
-        in_specs=[ANY] + [VMEM] * 6,
-        out_specs=[ANY, VMEM, VMEM],
-        out_shape=[jax.ShapeDtypeStruct(spectrum.shape, f32), square, square],
-        scratch_shapes=[
-            pltpu.VMEM((ndir, nfreq, width + 2 * LANES), f32),
-            pltpu.VMEM((ndir, nfreq, width), f32),
-            pltpu.VMEM((ndir, rows, 2 * width + 4 * LANES), jnp.bfloat16),
-            pltpu.SemaphoreType.DMA((blocks,)),
-            pltpu.SemaphoreType.DMA((blocks,)),
-        ],
-        compiler_params=params,
-        cost_estimate=pl.CostEstimate(
-            flops=30 * spectrum.size, bytes_accessed=8 * spectrum.size, transcendentals=0
-        ),
-    )(spectrum, before, after, neighbours, sea_mask.reshape(blocks, LANES), wind_u, wind_v)
+    scratch = [
+        pltpu.VMEM((ndir, nfreq, width + 2 * LANES), f32),
+        pltpu.VMEM((ndir, nfreq, width), f32),
+        pltpu.VMEM((ndir, rows, 2 * width + 4 * LANES), jnp.bfloat16),
+        pltpu.SemaphoreType.DMA((blocks,)),
+        pltpu.SemaphoreType.DMA((blocks,)),
+    ]
+    waves = [jax.ShapeDtypeStruct(spectrum.shape, f32), square, square]
+    shared = (spectrum, neighbours, sea_mask.reshape(blocks, LANES), wind_u, wind_v)
+
+    def wave(edge, *first):
+        return pl.pallas_call(
+            functools.partial(wave_kernel, edge),
+            in_specs=[VMEM, VMEM, ANY] * edge + [ANY] + [VMEM] * 4,
+            out_specs=[ANY, VMEM, VMEM],
+            out_shape=waves,
+            scratch_shapes=scratch,
+            input_output_aliases={2: 0} if edge else {},
+            cost_estimate=pl.CostEstimate(
+                flops=30 * spectrum.size, bytes_accessed=8 * spectrum.size, transcendentals=0
+            ),
+            **plain,
+        )(*first, *shared)
+
+    inner, logz, tau = wave(False)
+    spectrum_new, edge_logz, edge_tau = wave(True, before, after, inner)
+    row = lax.broadcasted_iota(jnp.int32, (blocks, LANES), 0)
+    inside = jnp.logical_and(row > 0, row < blocks - 1)
+    logz = jnp.where(inside, logz, edge_logz)
+    tau = jnp.where(inside, tau, edge_tau)
     rough, stress = unpack(exchange(1, pack(wave_source, logz, tau))[0])
     spectrum_new = spectrum_new.transpose(1, 0, 2)
     return (u_new, v_new, spectrum_new, rough.reshape(columns), stress.reshape(columns))

time: 54.8 us -> 52.5 us (0.958)
  Pallas kernels: 53.7 us -> 46 us
  starting transfers between devices: 0 us -> 5.4 us
    pallas_call x2, Pallas kernels: 30.3 us -> 19.8 us  [exchange(): pl.pallas_call(functools.partial(exchange_kernel, devices, lax.axis_size(...]
    ppermute x0 -> x2, starting transfers between devices: none -> 5.4 us  [the longest x1 3.86 us: local(): after = lax.ppermute(head, AXES, [(b, a) for a, b in up])]
    pallas_call x1 -> x2, Pallas kernels: 17.7 us -> 20.4 us  [wave(): pl.pallas_call(functools.partial(wave_kernel, edge), in_specs=[VMEM, VMEM...]
  transfers between devices with their start and end apart: 0 -> 2, of which waited for: 0 -> 0; matrix products, arithmetic and copies ran while one was open for 0% -> 0% of each run, Pallas kernels for 0% -> 33%
where the time goes in v4:
time: 52.5 us; the launch traced here: 52.3 us
  Pallas kernels  46 us (88%)
  starting transfers between devices  5.4 us (10%)
  between operations  0.83 us (2%)
    pallas_call x2, Pallas kernels, wave(): pl.pallas_call(functools.partial(wave_kernel, edge), in_specs=[VMEM, VMEM...  20.4 us
    pallas_call x2, Pallas kernels, exchange(): pl.pallas_call(functools.partial(exchange_kernel, devices, lax.axis_size(...  19.8 us
    ppermute x1, starting transfers between devices, local(): after = lax.ppermute(head, AXES, [(b, a) for a, b in up])  3.86 us
    pallas_call x2, Pallas kernels, pack(): pl.pallas_call(pack_kernel, in_specs=[VMEM] * 3, out_specs=VMEM, out_shap...  1.62 us
    pallas_call x1, Pallas kernels, local(): pl.pallas_call(rim_kernel, grid=(1,), in_specs=[edge(0), edge(width // LA...  1.57 us
    ppermute x1, starting transfers between devices, local(): before = lax.ppermute(tail, AXES, up)  1.54 us
    pallas_call x2, Pallas kernels, unpack(): pl.pallas_call(unpack_kernel, in_specs=[VMEM], out_specs=[VMEM] * 2, out_...  1.47 us
    pallas_call x1, Pallas kernels, local(): pl.pallas_call(solve_kernel, in_specs=[VMEM] * 4, out_specs=[VMEM] * 2, o...  1.07 us
  transfers between devices with their start and end apart: 2, of which 0 were waited for; matrix products, arithmetic and copies ran while one was open for 0% of the time, Pallas kernels for 33%

profile of v4, /device:TPU:0, one launch (start us, length us, event | category | flops | bytes accessed | tf_op | source)
XLA Modules:
  0.0 52.3 jit_solution(16032393076051668674)
XLA Ops:
  0.6 0.0 copy-start
  0.6 0.0 copy-start.1
  0.7 0.0 copy-start.6
  0.7 0.0 copy-start.2
  0.7 0.0 copy-start.5
  0.7 0.0 copy-start.3
  0.7 0.0 copy-start.4
  0.7 1.6 %shard_map.131 = (f32[18,29,128]{2,1,0:T(8,128)S(1)}, f32[18,29,128]{2,1,0:T(8,128)S(1)}) custom-call(f32[36,29,2048]{2,1,0:T(8,128)} %bitcast.17, f32[36,29,2048]{2,1,0:T(8,128)} %bitcast.18), custom_call_target="tpu_custom_call" | custom-call | tf_op jit(solution)/shard_map/pallas_call | solution.py:376
  2.3 0.0 copy-done
  2.3 0.0 copy-done.1
  2.3 0.0 copy-done.6
  2.3 0.8 %shard_map.129.refs_0_ = f32[32,4,128]{2,1,0:T(4,128)S(1)} custom-call(s32[16,128]{1,0:T(8,128)S(1)} %bitcast.15, f32[16,128]{1,0:T(8,128)S(1)} %bitcast.12, f32[16,128]{1,0:T(8,128)S(1)} %bitcast.13), custom_call_target="tpu_custom_call" | custom-call | tf_op jit(solution)/shard_map/pallas_call | solution.py:403
  3.2 11.2 %shard_map.130.inbox = f32[32,4,128]{2,1,0:T(4,128)S(1)} custom-call(f32[32,4,128]{2,1,0:T(4,128)S(1)} %shard_map.129.refs_0_), custom_call_target="tpu_custom_call" | custom-call | tf_op jit(solution)/shard_map/pallas_call | solution.py:391
  14.3 1.5 %collective-permute-start = (f32[18,29,128]{2,1,0:T(8,128)S(1)}, f32[18,29,128]{2,1,0:T(8,128)S(1)}, u32[]{:S(2)}, u32[]{:S(2)}) collective-permute-start(f32[18,29,128]{2,1,0:T(8,128)S(1)} %get-tuple-element.26), channel_id=1, source_target_pairs={{0,1},{1,2},{2,3},{3,4},{4,5},{5,6},{6,7},{7,8},{8,9},{9,10},{10,1... | collective-permute-start | bytes 801800 | tf_op jit(solution)/shard_map/ppermute | solution.py:416
  15.9 3.9 %collective-permute-start.1 = (f32[18,29,128]{2,1,0:T(8,128)S(1)}, f32[18,29,128]{2,1,0:T(8,128)S(1)}, u32[]{:S(2)}, u32[]{:S(2)}) collective-permute-start(f32[18,29,128]{2,1,0:T(8,128)S(1)} %get-tuple-element.27), channel_id=1, source_target_pairs={{1,0},{2,1},{3,2},{4,3},{5,4},{6,5},{7,6},{8,7},{9,8},{10,9},{11,1... | collective-permute-start | bytes 801800 | tf_op jit(solution)/shard_map/ppermute | solution.py:417
  19.7 0.4 shard_map.132
  20.2 0.0 copy-done.2
  20.2 0.0 copy-done.5
  20.2 1.1 %shard_map.128 = (f32[20,2048]{1,0:T(8,128)}, f32[20,2048]{1,0:T(8,128)}) custom-call(f32[20,2048]{1,0:T(8,128)S(1)} %copy-done, f32[20,2048]{1,0:T(8,128)S(1)} %copy-done.1, f32[19,2048]{1,0:T(8,128)S(1)} %copy-done.2, f32[1,2048]{1,0:T(1,128)S(1)} %bitcast.14), custom_call_target="tpu_custom_call" | custom-call | flops 819200 | bytes 819200 | tf_op jit(solution)/shard_map/pallas_call | solution.py:420
  21.3 0.0 copy-done.3
  21.3 0.0 copy-done.4
  21.3 15.8 %shard_map.133 = (f32[36,29,2048]{2,1,0:T(8,128)}, f32[16,128]{1,0:T(8,128)S(1)}, f32[16,128]{1,0:T(8,128)S(1)}) custom-call(f32[36,29,2048]{2,1,0:T(8,128)} %bitcast.19, s32[4,2048]{1,0:T(4,128)S(1)} %copy-done.3, s32[16,128]{1,0:T(8,128)S(1)} %bitcast.10, f32[16,128]{1,0:T(8,128)S(1)} %get-tuple-element.29.refs_3_.refs_6_, ...), custom_call_target="tpu_custom_call" | custom-call | flops 64143360 | bytes 17104896 | tf_op jit(solution)/shard_map/pallas_call | solution.py:439
  37.1 0.0 collective-permute-done.refs_0_
  37.1 0.0 collective-permute-done.1.refs_1_
  37.2 0.0 copy-start.7
  37.2 4.6 %shard_map.134 = (f32[36,29,2048]{2,1,0:T(8,128)}, f32[16,128]{1,0:T(8,128)S(1)}, f32[16,128]{1,0:T(8,128)S(1)}) custom-call(f32[18,29,128]{2,1,0:T(8,128)S(1)} %collective-permute-done.refs_0_, f32[18,29,128]{2,1,0:T(8,128)S(1)} %collective-permute-done.1.refs_1_, f32[36,29,2048]{2,1,0:T(8,128)} %get-tuple-element.31.refs_2_, ...), custom_call_target="tpu_custom_call", output_to_operand_aliasing={{0}: (2, {})} | custom-call | flops 64143360 | bytes 17104896 | tf_op jit(solution)/shard_map/pallas_call | solution.py:439
  41.7 0.1 broadcast_select_fusion
  41.8 0.0 copy-done.7
  41.8 0.8 %shard_map.135.refs_0_ = f32[32,4,128]{2,1,0:T(4,128)S(1)} custom-call(s32[16,128]{1,0:T(8,128)S(1)} %bitcast.16, f32[16,128]{1,0:T(8,128)S(1)} %get-tuple-element.40.first, f32[16,128]{1,0:T(8,128)S(1)} %get-tuple-element.39.second), custom_call_target="tpu_custom_call" | custom-call | tf_op jit(solution)/shard_map/pallas_call | solution.py:403
  42.6 8.6 %shard_map.136.inbox = f32[32,4,128]{2,1,0:T(4,128)S(1)} custom-call(f32[32,4,128]{2,1,0:T(4,128)S(1)} %shard_map.135.refs_0_), custom_call_target="tpu_custom_call" | custom-call | tf_op jit(solution)/shard_map/pallas_call | solution.py:391
  51.3 1.0 %shard_map.137 = (f32[16,128]{1,0:T(8,128)}, f32[16,128]{1,0:T(8,128)}) custom-call(f32[32,4,128]{2,1,0:T(4,128)S(1)} %shard_map.136.inbox), custom_call_target="tpu_custom_call" | custom-call | tf_op jit(solution)/shard_map/pallas_call | solution.py:408
  (3 shorter events, 0.0 us)
Async XLA Ops:
  0.6 1.7 %copy-start = (f32[20,2048]{1,0:T(8,128)S(1)}, f32[20,2048]{1,0:T(8,128)}, u32[]{:S(2)}) copy-start(f32[20,2048]{1,0:T(8,128)} %u_ref.1) | copy-start | bytes 491524
  0.6 1.7 %copy-start.1 = (f32[20,2048]{1,0:T(8,128)S(1)}, f32[20,2048]{1,0:T(8,128)}, u32[]{:S(2)}) copy-start(f32[20,2048]{1,0:T(8,128)} %v_ref.1) | copy-start | bytes 491524
  0.7 1.7 %copy-start.6 = (s32[2048]{0:T(1024)S(1)}, s32[2048]{0:T(1024)}, u32[]{:S(2)}) copy-start(s32[2048]{0:T(1024)} %param.16) | copy-start | bytes 24580
  0.7 19.5 %copy-start.2 = (f32[19,2048]{1,0:T(8,128)S(1)}, f32[19,2048]{1,0:T(8,128)}, u32[]{:S(2)}) copy-start(f32[19,2048]{1,0:T(8,128)} %mixing.1) | copy-start | bytes 466948
  0.7 19.5 %copy-start.5 = (f32[2048]{0:T(1024)S(1)}, f32[2048]{0:T(1024)}, u32[]{:S(2)}) copy-start(f32[2048]{0:T(1024)} %param.12) | copy-start | bytes 24580
  0.7 20.6 %copy-start.3 = (s32[4,2048]{1,0:T(4,128)S(1)}, s32[4,2048]{1,0:T(4,128)}, u32[]{:S(2)}) copy-start(s32[4,2048]{1,0:T(4,128)} %refs_4_.1) | copy-start | bytes 98308
  0.7 20.6 %copy-start.4 = (s32[2048]{0:T(1024)S(1)}, s32[2048]{0:T(1024)}, u32[]{:S(2)}) copy-start(s32[2048]{0:T(1024)} %param.14) | copy-start | bytes 24580
  14.3 22.8 %collective-permute-start = (f32[18,29,128]{2,1,0:T(8,128)S(1)}, f32[18,29,128]{2,1,0:T(8,128)S(1)}, u32[]{:S(2)}, u32[]{:S(2)}) collective-permute-start(f32[18,29,128]{2,1,0:T(8,128)S(1)} %get-tuple-element.26), channel_id=1, source_target_pairs={{0,1},{1,2},{2,3},{3,4},{4,5},{5,6},{6,7},{7,8},{8,9},{9,10},{10,1... | collective-permute-start | bytes 801800 | tf_op jit(solution)/shard_map/ppermute | solution.py:416
  15.9 21.3 %collective-permute-start.1 = (f32[18,29,128]{2,1,0:T(8,128)S(1)}, f32[18,29,128]{2,1,0:T(8,128)S(1)}, u32[]{:S(2)}, u32[]{:S(2)}) collective-permute-start(f32[18,29,128]{2,1,0:T(8,128)S(1)} %get-tuple-element.27), channel_id=1, source_target_pairs={{1,0},{2,1},{3,2},{4,3},{5,4},{6,5},{7,6},{8,7},{9,8},{10,9},{11,1... | collective-permute-start | bytes 801800 | tf_op jit(solution)/shard_map/ppermute | solution.py:417
  37.2 4.7 %copy-start.7 = (s32[2048]{0:T(1024)S(1)}, s32[2048]{0:T(1024)}, u32[]{:S(2)}) copy-start(s32[2048]{0:T(1024)} %param.15) | copy-start | bytes 24580
